TPU v7x, 32 devices: a whole 2x2x4 slice. The times are simulated.
32 devices in a mesh: mode: 16 (over z, y, core), tile: 2 (over x).
Axes of the slice: x: 2, y: 2, z: 4, core: 2. Of those that a mesh axis runs over, the one named last changes fastest.
Arguments:
- fluid_temp: bfloat16 [1024, 256, 512], P('mode', 'tile'), may hold values from -6 to 6
- solid_temp: float32 [2, 512, 64, 1024], P(None, 'mode', None, 'tile'), may hold values from -6 to 6
- material: int32 [2, 512, 64, 1024], P(None, 'mode', None, 'tile'), may hold values from 0 to 3
Outputs:
- fluid_modes: float32 [1024, 256, 512], P(('mode', 'tile'))
- solid_next: float32 [2, 512, 64, 1024], P(None, 'mode', None, 'tile')
All inputs are finite; a program needn't handle non-finite values.
Results may differ from a plain program's by a relative error of at most 0.0003.
Values may be sent and summed in bfloat16 or wider, within the bound.
A program may use at most 192 MiB of HBM per device.

v0:
```python
import math

import jax
import jax.numpy as jnp
from jax import lax
from jax.sharding import PartitionSpec as P

NZ = 1024
NY = 256
NX = 512
SUBSTEPS = 4


SIGMA = 0.1
SOLID_STEP = 0.04
HIGHEST = lax.Precision.HIGHEST


def padded_2(array, sides, width):
    for axis, dim in sides:
        size, length = (lax.axis_size(axis), array.shape[dim])
        up = [(i, (i + 1) % size) for i in range(size)]
        down = [(j, i) for i, j in up]
        last = lax.slice_in_dim(array, length - width, length, axis=dim)
        first = lax.slice_in_dim(array, 0, width, axis=dim)
        before = lax.ppermute(last, axis, up)
        after = lax.ppermute(first, axis, down)
        array = jnp.concatenate([before, array, after], axis=dim)
    return array


def fourier_rows(length, row_ids):
    col_ids = jnp.arange(length, dtype=jnp.int32)[None, :]
    row_ids = row_ids[:, None]
    wave_num = (row_ids + 1) // 2
    angles = (wave_num * col_ids % length).astype(jnp.float32) * (2.0 * math.pi / length)
    factor = jnp.where(
        (wave_num == 0) | (2 * wave_num == length), math.sqrt(1.0 / length), math.sqrt(2.0 / length)
    )
    return factor * jnp.where((row_ids % 2 == 1) | (row_ids == 0), jnp.cos(angles), jnp.sin(angles))


def fourier_eigen(length, row_ids):
    wave_num = (row_ids + 1) // 2
    return 2.0 - 2.0 * jnp.cos(wave_num.astype(jnp.float32) * (2.0 * math.pi / length))


def sine_table(length):
    row_ids = jnp.arange(length, dtype=jnp.int32)[:, None]
    col_ids = jnp.arange(length, dtype=jnp.int32)[None, :]
    angles = ((row_ids + 1) * (col_ids + 1) % (2 * length + 2)).astype(jnp.float32) * (
        math.pi / (length + 1)
    )
    return math.sqrt(2.0 / (length + 1)) * jnp.sin(angles)


def sine_eigen(length):
    col_ids = jnp.arange(length, dtype=jnp.int32)
    return 2.0 - 2.0 * jnp.cos((col_ids + 1).astype(jnp.float32) * (math.pi / (length + 1)))


def conductivity(material):
    return jnp.where(
        material == 0, 0.5, jnp.where(material == 1, 1.0, jnp.where(material == 2, 2.0, 4.0))
    ).astype(jnp.float32)


def harmonic(first, second):
    return 2.0 * first * second / (first + second)


def helmholtz(spectra, span_eigen, wall_vecs, wall_eigen, stream_vecs, stream_eigen):
    coeffs = jnp.einsum("myx,yq->mqx", spectra, wall_vecs, precision=HIGHEST)
    coeffs = jnp.einsum("mqx,px->mqp", coeffs, stream_vecs, precision=HIGHEST)
    coeffs = coeffs / (
        SIGMA + span_eigen[:, None, None] + wall_eigen[None, :, None] + stream_eigen[None, None, :]
    )
    coeffs = jnp.einsum("mqp,px->mqx", coeffs, stream_vecs, precision=HIGHEST)
    return jnp.einsum("mqx,yq->myx", coeffs, wall_vecs, precision=HIGHEST)


def substep(padded, conduct_pad, wall_flux):
    centre = padded[:, 1:-1, :, 1:-1]
    conduct = conduct_pad[:, 1:-1, :, 1:-1]
    divergence = jnp.zeros_like(centre)
    neighbours = (
        (padded[:, 2:, :, 1:-1], conduct_pad[:, 2:, :, 1:-1]),
        (padded[:, :-2, :, 1:-1], conduct_pad[:, :-2, :, 1:-1]),
        (padded[:, 1:-1, :, 2:], conduct_pad[:, 1:-1, :, 2:]),
        (padded[:, 1:-1, :, :-2], conduct_pad[:, 1:-1, :, :-2]),
    )
    for near_heat, near_cond in neighbours:
        divergence = divergence + harmonic(near_cond, conduct) * (near_heat - centre)
    normal = harmonic(conduct[:, :, 1:, :], conduct[:, :, :-1, :]) * (
        centre[:, :, 1:, :] - centre[:, :, :-1, :]
    )
    divergence = (
        divergence
        + jnp.pad(normal, ((0, 0), (0, 0), (0, 1), (0, 0)))
        - jnp.pad(normal, ((0, 0), (0, 0), (1, 0), (0, 0)))
    )
    divergence = divergence.at[:, :, 0, :].add(wall_flux)
    return centre + SOLID_STEP * divergence


def per_device(fluid_temp, solid_temp, material):
    n_mode = lax.axis_size("mode")
    n_tile = lax.axis_size("tile")
    mode_idx = lax.axis_index("mode")
    tile_idx = lax.axis_index("tile")
    per_dev = NZ // (n_mode * n_tile)
    x_rows = solid_temp.shape[1]
    z_cols = solid_temp.shape[3]
    own_modes = (mode_idx * n_tile + tile_idx) * per_dev + jnp.arange(per_dev, dtype=jnp.int32)
    wall_temp = solid_temp[:, :, 0, :]
    tile_ids = jnp.arange(n_tile, dtype=jnp.int32)
    mode_ids = jnp.arange(n_mode, dtype=jnp.int32)
    own_split = fourier_rows(NZ, own_modes).reshape(per_dev, n_tile, z_cols)

    def selectors(amount):
        blocks = jnp.arange(amount, dtype=jnp.int32)
        pick_z = (blocks[:, None] % n_tile == tile_ids[None, :]).astype(jnp.float32)
        pick_x = (blocks[:, None] // n_tile == mode_ids[None, :]).astype(jnp.float32)
        return (jnp.einsum("kt,mtz->kmz", pick_z, own_split, precision=HIGHEST), pick_x)

    pieces = lax.all_gather(wall_temp[None], ("mode", "tile"), axis=0, tiled=True)
    picked, pick_x = selectors(pieces.shape[0])
    partial_sum = jnp.einsum("kmz,kwxz->wmkx", picked, pieces, precision=HIGHEST)
    wall_hat = jnp.einsum("wmkx,kb->wmbx", partial_sum, pick_x, precision=HIGHEST).reshape(
        2, per_dev, NX
    )
    span_table = fourier_rows(NZ, jnp.arange(NZ, dtype=jnp.int32))
    scaled = SIGMA * lax.all_to_all(
        fluid_temp, "mode", split_axis=1, concat_axis=0, tiled=True
    ).astype(jnp.float32)
    coeffs = jnp.einsum("mz,zyx->myx", span_table, scaled, precision=HIGHEST)
    regrouped = lax.all_to_all(
        lax.all_to_all(coeffs, "mode", split_axis=0, concat_axis=1, tiled=True),
        "tile",
        split_axis=0,
        concat_axis=1,
        tiled=True,
    )
    spectra = regrouped
    spectra = spectra.at[:, 0, :].add(wall_hat[0]).at[:, NY - 1, :].add(wall_hat[1])
    stream_ids = jnp.arange(NX, dtype=jnp.int32)
    fluid_modes = helmholtz(
        spectra,
        fourier_eigen(NZ, own_modes),
        sine_table(NY),
        sine_eigen(NY),
        fourier_rows(NX, stream_ids),
        fourier_eigen(NX, stream_ids),
    )
    near_hat = jnp.stack([fluid_modes[:, 0, :], fluid_modes[:, NY - 1, :]])
    near_split = near_hat.reshape(2, per_dev, n_mode, x_rows)
    picked, pick_x = selectors(lax.axis_size(("mode", "tile")) * 1)
    columns = jnp.einsum("kb,wmbx->kwmx", pick_x, near_split, precision=HIGHEST)
    fluid_side = lax.psum_scatter(
        jnp.einsum("kwmx,kmz->kwxz", columns, picked, precision=HIGHEST),
        ("mode", "tile"),
        scatter_dimension=0,
        tiled=True,
    )[0]
    wall_flux = fluid_side - wall_temp
    conduct = conductivity(material)
    thermal = solid_temp
    for substep_id in range(SUBSTEPS):
        padded = padded_2(jnp.stack([thermal, conduct]), (("mode", 2), ("tile", 4)), 1)
        thermal = substep(padded[0], padded[1], wall_flux)
    return (fluid_modes, thermal)


def solution(mesh):
    placed = (P("mode", "tile", None), P(None, "mode", None, "tile"), P(None, "mode", None, "tile"))
    return jax.shard_map(
        per_device,
        mesh=mesh,
        in_specs=placed,
        out_specs=(P(("mode", "tile"), None, None), P(None, "mode", None, "tile")),
        check_vma=False,
    )
```

profile of v0, /device:TPU:1, one launch (start us, length us, event | category | flops | bytes accessed | tf_op | source)
XLA Modules:
  0.0 1807.9 jit_solution(13783159265130998404)
XLA Ops:
  26.1 19.2 %fusion.241 = f32[1024,1024,1]{1,0,2:T(8,128)} fusion(s32[1024]{0:T(1024)S(1)} %add_select_fusion.4, f32[1024]{0:T(1024)S(1)} %fusion.173, pred[1024]{0:T(1024)(128)(4,1)S(1)} %fusion.174), kind=kLoop, calls=%fused_computation.127.clone.1 | loop fusion | flops 16777216 | bytes 4203520 | tf_op jit(solution)/shard_map/mz,zyx->myx/dot_general | solution.py:136
  45.3 131.9 %all-to-all-done = bf16[64,128,512]{2,0,1:T(8,128)(2,1)} async-done(((bf16[64,128,512]{2,0,1:T(8,128)(2,1)}), bf16[64,128,512]{2,0,1:T(8,128)(2,1)}, u32[]{:S(2)}, u32[]{:S(2)}) %all-to-all-start) | async-done | bytes 8388640 | tf_op jit(solution)/shard_map/all_to_all | solution.py:133
  196.7 56.4 %fusion.74 = f32[1024,8,512]{2,0,1:T(8,128)} fusion(f32[1024,8,512]{2,0,1:T(8,128)S(1)} %bitcast.111, f32[1024,1024,1]{1,0,2:T(8,128)S(1)} %copy-done.9), kind=kOutput, calls=%fused_computation.126 | convolution fusion | flops 51539607552 | bytes 37748736 | tf_op jit(solution)/shard_map/mz,zyx->myx/dot_general | solution.py:136
  271.0 36.1 %all-to-all-start.1 = ((f32[1024,8,512]{2,1,0:T(8,128)}), f32[1024,8,512]{2,1,0:T(8,128)}, u32[]{:S(2)}, u32[]{:S(2)}) async-start(f32[1024,8,512]{2,1,0:T(8,128)} %copy.74), calls=%async_computation.1 | async-start | bytes 33554432 | tf_op jit(solution)/shard_map/all_to_all | solution.py:138
  319.5 304.6 %all-to-all-done.1 = f32[1024,8,512]{2,1,0:T(8,128)} async-done(((f32[1024,8,512]{2,1,0:T(8,128)}), f32[1024,8,512]{2,1,0:T(8,128)}, u32[]{:S(2)}, u32[]{:S(2)}) %all-to-all-start.1) | async-done | bytes 16777248 | tf_op jit(solution)/shard_map/all_to_all | solution.py:138
  659.7 22.4 %collective-permute-start = (f32[2,2,1,64,512]{4,2,1,3,0:T(1,128)}, f32[2,2,1,64,512]{4,2,1,3,0:T(1,128)}, u32[]{:S(2)}, u32[]{:S(2)}) collective-permute-start(f32[2,2,1,64,512]{4,2,1,3,0:T(1,128)} %get-tuple-element.88), channel_id=1, source_target_pairs={{0,2},{2,4},{4,6},{6,8},{8,10},{10,12},{12,14},{14,16},{16,18},{18... | collective-permute-start | bytes 1572872 | tf_op jit(solution)/shard_map/ppermute | solution.py:26
  730.4 100.9 %collective-permute-done.2 = f32[2,2,34,64,1]{3,1,4,2,0:T(2,128)S(1)} collective-permute-done((f32[2,2,34,64,1]{3,1,4,2,0:T(2,128)S(1)}, f32[2,2,34,64,1]{3,1,4,2,0:T(2,128)S(1)}, u32[]{:S(2)}, u32[]{:S(2)}) %collective-permute-start.2) | collective-permute-done | bytes 34848 | tf_op jit(solution)/shard_map/ppermute | solution.py:26
  838.3 25.8 %fusion.3 = f32[2,2,34,64,514]{4,2,1,3,0:T(8,128)} fusion(f32[1,2,32,64,512]{4,2,1,3,0:T(8,128)} %copy-done, f32[2,2,34,64,1]{4,2,1,3,0:T(8,128)} %copy.91, f32[2,2,1,64,512]{4,2,1,3,0:T(1,128)} %collective-permute-done.1, f32[1,2,32,64,512]{4,2,1,3,0:T(8,128)} %bitcast.105, f32[2,2,1,64,512]{4,2,1,3,0:T(1,128)} %collective-permute-done, ...), kind=kLoop, calls=%fused_computation.11 | loop fusion | flops 22369280 | bytes 35790848 | tf_op jit(solution)/shard_map/concatenate | solution.py:28
  897.6 24.6 %fusion.126 = f32[256,32,512]{2,0,1:T(8,128)} fusion(f32[32,256,512]{2,1,0:T(8,128)} %scatter-add.21, s32[256]{0:T(256)S(1)} %iota_add_fusion.2), kind=kOutput, calls=%fused_computation.187 | convolution fusion | flops 12885557248 | bytes 33555456 | tf_op jit(solution)/shard_map/myx,yq->mqx/dot_general | solution.py:73
  922.2 32.3 %fusion.24 = f32[32,256,512]{2,1,0:T(8,128)S(1)} fusion(f32[256,32,512]{2,0,1:T(8,128)} %fusion.126, f32[512,512,1]{1,0,2:T(8,128)S(1)} %fusion.237), kind=kOutput, calls=%fused_computation.32 | convolution fusion | flops 25769803776 | bytes 34603008 | tf_op jit(solution)/shard_map/mqx,px->mqp/dot_general | solution.py:74
  954.6 31.2 %fusion.26 = f32[32,256,512]{2,1,0:T(8,128)} fusion(f32[32,256,512]{2,1,0:T(8,128)S(1)} %fusion.24, f32[512]{0:T(512)S(1)} %get-tuple-element.122, f32[32,256]{1,0:T(8,128)S(1)} %copy-done.11, f32[512,512,1]{1,0,2:T(8,128)S(1)} %copy-done.10), kind=kOutput, calls=%fused_computation.35 | convolution fusion | flops 25778192384 | bytes 34637824 | tf_op jit(solution)/shard_map/mqp,px->mqx/dot_general | solution.py:78
  985.8 24.2 %convolution_bitcast_fusion = f32[32,256,512]{2,1,0:T(8,128)} fusion(f32[32,256,512]{2,1,0:T(8,128)} %fusion.26, s32[256]{0:T(256)S(1)} %iota_add_fusion.2), kind=kOutput, calls=%fused_computation.52 | convolution fusion | flops 12885557248 | bytes 33555456 | tf_op jit(solution)/shard_map/mqx,yq->myx/dot_general | solution.py:79
  1036.4 23.4 %fusion.70 = f32[2,32,63,512]{3,1,0,2:T(8,128)} fusion(f32[2,34,64,514]{3,1,0,2:T(8,128)} %get-tuple-element.99, f32[2,34,64,514]{3,1,0,2:T(8,128)} %get-tuple-element.98), kind=kLoop, calls=%fused_computation.119 | loop fusion | flops 12386304 | bytes 41287680 | tf_op jit(solution)/shard_map/mul | solution.py:94
  1059.9 59.5 %fusion.59 = f32[2,32,64,512]{3,1,0,2:T(8,128)} fusion(f32[2,34,64,514]{3,1,0,2:T(8,128)} %get-tuple-element.99, f32[2,32,63,512]{3,1,0,2:T(8,128)} %fusion.70, f32[2,34,64,514]{3,1,0,2:T(8,128)} %get-tuple-element.98), kind=kLoop, calls=%fused_computation.96 | loop fusion | flops 60817408 | bytes 100532224 | tf_op jit(solution)/shard_map/sub | solution.py:98
  1119.4 103.5 %reduce-scatter.2.cloned.1.call-done = f32[1,2,32,512]{3,2,1,0:T(8,128)} async-done(((f32[32,2,32,512]{3,2,1,0:T(8,128)}), f32[1,2,32,512]{3,2,1,0:T(8,128)}) %reduce-scatter.2.cloned.1.call-update) | async-done | bytes 131088 | tf_op jit(solution)/shard_map/reduce_scatter | solution.py:159
  1292.5 24.3 %fusion.7 = f32[2,2,34,64,514]{4,2,1,3,0:T(8,128)S(1)} fusion(f32[1,2,32,64,512]{4,2,1,3,0:T(8,128)} %copy-done, f32[2,2,34,64,1]{4,2,1,3,0:T(8,128)} %copy.97, f32[2,2,1,64,512]{4,2,1,3,0:T(1,128)S(1)} %collective-permute-done.5, f32[1,2,32,64,512]{4,2,1,3,0:T(8,128)} %add_bitcast_fusion.2, f32[2,2,1,64,512]{4,2,1,3,0:T(1,128)S(1)} %collective-permute-done.4, ...), kind=kLoop, calls=%fused_computation.15 | loop fusion | flops 22369280 | bytes 35790848 | tf_op jit(solution)/shard_map/concatenate | solution.py:28
  1325.9 23.4 %fusion.69 = f32[2,32,63,512]{3,1,0,2:T(8,128)} fusion(f32[2,34,64,514]{3,1,0,2:T(8,128)} %get-tuple-element.97, f32[2,34,64,514]{3,1,0,2:T(8,128)} %get-tuple-element.96), kind=kLoop, calls=%fused_computation.117 | loop fusion | flops 12386304 | bytes 41287680 | tf_op jit(solution)/shard_map/mul | solution.py:94
  1349.4 57.5 %fusion.50 = f32[2,32,64,512]{3,1,0,2:T(8,128)} fusion(f32[2,34,64,514]{3,1,0,2:T(8,128)} %get-tuple-element.97, f32[2,32,63,512]{3,1,0,2:T(8,128)} %fusion.69, f32[2,34,64,514]{3,1,0,2:T(8,128)} %get-tuple-element.96), kind=kLoop, calls=%fused_computation.83 | loop fusion | flops 60817408 | bytes 100532224 | tf_op jit(solution)/shard_map/sub | solution.py:98
  1476.6 24.3 %fusion.11 = f32[2,2,34,64,514]{4,2,1,3,0:T(8,128)S(1)} fusion(f32[1,2,32,64,512]{4,2,1,3,0:T(8,128)} %copy-done, f32[2,2,34,64,1]{4,2,1,3,0:T(8,128)} %copy.101, f32[2,2,1,64,512]{4,2,1,3,0:T(1,128)S(1)} %collective-permute-done.9, f32[1,2,32,64,512]{4,2,1,3,0:T(8,128)} %add_bitcast_fusion.1, f32[2,2,1,64,512]{4,2,1,3,0:T(1,128)S(1)} %collective-permute-done.8, ...), kind=kLoop, calls=%fused_computation.19 | loop fusion | flops 22369280 | bytes 35790848 | tf_op jit(solution)/shard_map/concatenate | solution.py:28
  1510.1 23.7 %fusion.68 = f32[2,32,63,512]{3,1,0,2:T(8,128)} fusion(f32[2,34,64,514]{3,1,0,2:T(8,128)} %get-tuple-element.95, f32[2,34,64,514]{3,1,0,2:T(8,128)} %get-tuple-element.94), kind=kLoop, calls=%fused_computation.115 | loop fusion | flops 12386304 | bytes 41287680 | tf_op jit(solution)/shard_map/mul | solution.py:94
  1533.7 57.5 %fusion.41 = f32[2,32,64,512]{3,1,0,2:T(8,128)} fusion(f32[2,34,64,514]{3,1,0,2:T(8,128)} %get-tuple-element.95, f32[2,32,63,512]{3,1,0,2:T(8,128)} %fusion.68, f32[2,34,64,514]{3,1,0,2:T(8,128)} %get-tuple-element.94), kind=kLoop, calls=%fused_computation.70 | loop fusion | flops 60817408 | bytes 100532224 | tf_op jit(solution)/shard_map/sub | solution.py:98
  1660.5 24.3 %fusion.15 = f32[2,2,34,64,514]{4,2,1,3,0:T(8,128)S(1)} fusion(f32[1,2,32,64,512]{4,2,1,3,0:T(8,128)} %copy-done, f32[2,2,34,64,1]{4,2,1,3,0:T(8,128)} %copy.105, f32[2,2,1,64,512]{4,2,1,3,0:T(1,128)S(1)} %collective-permute-done.13, f32[1,2,32,64,512]{4,2,1,3,0:T(8,128)} %add_bitcast_fusion, f32[2,2,1,64,512]{4,2,1,3,0:T(1,128)S(1)} %collective-permute-done.12, ...), kind=kLoop, calls=%fused_computation.23 | loop fusion | flops 22369280 | bytes 35790848 | tf_op jit(solution)/shard_map/concatenate | solution.py:28
  1693.9 23.4 %fusion.67 = f32[2,32,63,512]{3,1,0,2:T(8,128)} fusion(f32[2,34,64,514]{3,1,0,2:T(8,128)} %get-tuple-element.93, f32[2,34,64,514]{3,1,0,2:T(8,128)} %get-tuple-element.92), kind=kLoop, calls=%fused_computation.113 | loop fusion | flops 12386304 | bytes 41287680 | tf_op jit(solution)/shard_map/mul | solution.py:94
  1717.4 57.2 %fusion.32 = f32[2,32,64,512]{3,1,0,2:T(8,128)} fusion(f32[2,34,64,514]{3,1,0,2:T(8,128)} %get-tuple-element.93, f32[2,32,63,512]{3,1,0,2:T(8,128)} %fusion.67, f32[2,34,64,514]{3,1,0,2:T(8,128)} %get-tuple-element.92), kind=kLoop, calls=%fused_computation.57 | loop fusion | flops 60817408 | bytes 100532224 | tf_op jit(solution)/shard_map/sub | solution.py:98
  (144 shorter events, 481.4 us)
Async XLA Ops:
  18.7 158.5 %all-to-all-start = ((bf16[64,128,512]{2,0,1:T(8,128)(2,1)}), bf16[64,128,512]{2,0,1:T(8,128)(2,1)}, u32[]{:S(2)}, u32[]{:S(2)}) async-start(bf16[64,128,512]{2,0,1:T(8,128)(2,1)} %copy.72), calls=%async_computation | async-start | bytes 16777216 | tf_op jit(solution)/shard_map/all_to_all | solution.py:133
  271.0 353.1 %all-to-all-start.1 = ((f32[1024,8,512]{2,1,0:T(8,128)}), f32[1024,8,512]{2,1,0:T(8,128)}, u32[]{:S(2)}, u32[]{:S(2)}) async-start(f32[1024,8,512]{2,1,0:T(8,128)} %copy.74), calls=%async_computation.1 | async-start | bytes 33554432 | tf_op jit(solution)/shard_map/all_to_all | solution.py:138
  307.2 556.9 %all-gather.3.cloned.1.call-start = ((), (), s32[]{:S(2)}) async-start(), calls=%async_computation.5 | async-start | bytes 4325376 | tf_op jit(solution)/shard_map/all_gather | solution.py:126
  636.2 242.5 %all-to-all-start.2 = ((f32[64,128,512]{2,1,0:T(8,128)}), f32[64,128,512]{2,1,0:T(8,128)}, u32[]{:S(2)}, u32[]{:S(2)}) async-start(f32[64,128,512]{2,1,0:T(8,128)} %bitcast.109), calls=%async_computation.2 | async-start | bytes 33554432 | tf_op jit(solution)/shard_map/all_to_all | solution.py:137
  645.9 577.0 %reduce-scatter.2.cloned.1.call-start = ((), (), s32[]{:S(2)}) async-start(), calls=%async_computation.4 | async-start | bytes 4325376 | tf_op jit(solution)/shard_map/reduce_scatter | solution.py:159
  659.7 36.9 %collective-permute-start = (f32[2,2,1,64,512]{4,2,1,3,0:T(1,128)}, f32[2,2,1,64,512]{4,2,1,3,0:T(1,128)}, u32[]{:S(2)}, u32[]{:S(2)}) collective-permute-start(f32[2,2,1,64,512]{4,2,1,3,0:T(1,128)} %get-tuple-element.88), channel_id=1, source_target_pairs={{0,2},{2,4},{4,6},{6,8},{8,10},{10,12},{12,14},{14,16},{16,18},{18... | collective-permute-start | bytes 1572872 | tf_op jit(solution)/shard_map/ppermute | solution.py:26
  682.1 14.5 collective-permute-start.1
  728.7 106.1 %collective-permute-start.3 = (f32[2,2,34,64,1]{3,1,4,2,0:T(2,128)S(1)}, f32[2,2,34,64,1]{3,1,4,2,0:T(2,128)S(1)}, u32[]{:S(2)}, u32[]{:S(2)}) collective-permute-start(f32[2,2,34,64,1]{3,1,4,2,0:T(2,128)S(1)} %copy.89), channel_id=1, source_target_pairs={{1,0},{0,1},{3,2},{2,3},{5,4},{4,5},{7,6},{6,7},{9,8},{8,9},{11,10... | collective-permute-start | bytes 104456 | tf_op jit(solution)/shard_map/ppermute | solution.py:27
  730.4 101.0 %collective-permute-start.2 = (f32[2,2,34,64,1]{3,1,4,2,0:T(2,128)S(1)}, f32[2,2,34,64,1]{3,1,4,2,0:T(2,128)S(1)}, u32[]{:S(2)}, u32[]{:S(2)}) collective-permute-start(f32[2,2,34,64,1]{3,1,4,2,0:T(2,128)S(1)} %copy.88), channel_id=1, source_target_pairs={{0,1},{1,0},{2,3},{3,2},{4,5},{5,4},{6,7},{7,6},{8,9},{9,8},{10,11... | collective-permute-start | bytes 104456 | tf_op jit(solution)/shard_map/ppermute | solution.py:26
  922.2 32.3 %copy-start.10 = (f32[512,512,1]{1,0,2:T(8,128)S(1)}, f32[512,512,1]{1,0,2:T(8,128)}, u32[]{:S(2)}) copy-start(f32[512,512,1]{1,0,2:T(8,128)} %fusion.239) | copy-start | bytes 3145732
  922.2 32.4 %copy-start.11 = (f32[32,256]{1,0:T(8,128)S(1)}, f32[32,256]{1,0:T(8,128)}, u32[]{:S(2)}) copy-start(f32[32,256]{1,0:T(8,128)} %broadcast_add_fusion) | copy-start | bytes 98308
  1241.2 8.1 collective-permute-start.4
  1241.3 14.3 collective-permute-start.5
  1280.4 5.1 collective-permute-start.6
  1283.9 5.0 collective-permute-start.7
  1421.6 18.0 copy-start.5
  1424.9 6.6 collective-permute-start.8
  1425.4 14.2 collective-permute-start.9
  1464.5 5.1 collective-permute-start.10
  1468.5 4.6 collective-permute-start.11
  1609.3 6.6 collective-permute-start.12
  1609.7 13.8 collective-permute-start.13
  1648.4 5.1 collective-permute-start.14
  1652.4 4.5 collective-permute-start.15
  (9 other events, 92.5 us)
Sparse Core Ops, SparseCore 0:
  319.6 256.7 all-gather.2
  1019.5 203.3 reduce-scatter.1
where the time goes:
time: 1820 us; the launch traced here: 1810 us
  waiting for transfers between devices  680 us (37%)
  other arithmetic  601 us (33%)
  local copies, waits for them, and re-layouts  234 us (13%)
  matrix products  192 us (11%)
  starting transfers between devices  86.4 us (5%)
    all_to_all x1, waiting for transfers between devices, per_device(): lax.all_to_all(coeffs, 'mode', split_axis=0, concat_axis=1, tiled=True)  305 us
    sub x4, other arithmetic, substep(): divergence + jnp.pad(normal, ((0, 0), (0, 0), (0, 1), (0, 0)))  232 us
    concatenate x8, other arithmetic, padded_2(): array = jnp.concatenate([before, array, after], axis=dim)  150 us
    all_to_all x1, waiting for transfers between devices, per_device(): lax.all_to_all(fluid_temp, 'mode', split_axis=1, concat_axis=0, tiled=True)  132 us
    ppermute x8, waiting for transfers between devices, padded_2(): before = lax.ppermute(last, axis, up)  118 us
    reduce_scatter x1, waiting for transfers between devices, per_device(): lax.psum_scatter(jnp.einsum('kwmx,kmz->kwxz', columns, picked, precision=...  103 us
    mul x4, other arithmetic, substep(): harmonic(conduct[:, :, 1:, :], conduct[:, :, :-1, :])  94 us
    another operation x8, other arithmetic, per_device(): jnp.stack([thermal, conduct])  62.1 us
  transfers between devices with their start and end apart: 21, of which 10 were waited for; matrix products, arithmetic and copies ran while one was open for 15% of the time, Pallas kernels for 0%

commit v1 on v0

v1 whole, which is shorter than its diff:
```python
import functools
import math

import jax
import jax.numpy as jnp
import numpy as np
from jax import lax
from jax.experimental import pallas as pl
from jax.experimental.pallas import tpu as pltpu
from jax.sharding import PartitionSpec as P

SUBSTEPS = 4
SIGMA = 0.1
SOLID_STEP = 0.04
HIGHEST = lax.Precision.HIGHEST
LEVELS = 32767.0
BOTH = ("mode", "tile")


def fourier_table(length):
    rows = np.arange(length)[:, None]
    cols = np.arange(length)[None, :]
    wave_num = (rows + 1) // 2
    angles = (wave_num * cols % length) * (2.0 * math.pi / length)
    factor = np.where(
        (wave_num == 0) | (2 * wave_num == length), math.sqrt(1.0 / length), math.sqrt(2.0 / length)
    )
    return factor * np.where((rows % 2 == 1) | (rows == 0), np.cos(angles), np.sin(angles))


def fourier_eigen(length):
    wave_num = (np.arange(length) + 1) // 2
    return 2.0 - 2.0 * np.cos(wave_num * (2.0 * math.pi / length))


def sine_table(length):
    ids = np.arange(length) + 1
    angles = (ids[:, None] * ids[None, :] % (2 * length + 2)) * (math.pi / (length + 1))
    return math.sqrt(2.0 / (length + 1)) * np.sin(angles)


def sine_eigen(length):
    return 2.0 - 2.0 * np.cos((np.arange(length) + 1) * (math.pi / (length + 1)))


def split_table(table):
    high = table.astype(jnp.bfloat16)
    low = (table - high.astype(np.float64)).astype(jnp.bfloat16)
    return np.stack([high, low])


def split(value):
    high = value.astype(jnp.bfloat16)
    return high, (value - high.astype(jnp.float32)).astype(jnp.bfloat16)


def mm(first, second):
    return jnp.dot(first, second, preferred_element_type=jnp.float32)


def table_right(value, table):
    high, low = split(value)
    return mm(high, table[0]) + (mm(low, table[0]) + mm(high, table[1]))


def table_left(table, value):
    high, low = split(value)
    return mm(table[0], high) + (mm(table[0], low) + mm(table[1], high))


def span_kernel(rows_y, width, table_ref, fluid_ref, code_ref, scale_ref):
    lane = lax.broadcasted_iota(jnp.int32, scale_ref.shape, 1)
    scales = jnp.zeros(scale_ref.shape, jnp.float32)
    for row in range(rows_y):
        cols = pl.ds(row * width, width)
        fluid = fluid_ref[:, cols]
        spectra = mm(table_ref[0], fluid) + mm(table_ref[1], fluid)
        top = jnp.maximum(jnp.max(jnp.abs(spectra), axis=1, keepdims=True), 1e-30)
        code_ref[:, cols] = jnp.round(spectra * (LEVELS / top)).astype(jnp.int32).astype(jnp.int16)
        scales = jnp.where(lane == row, top * (1.0 / LEVELS), scales)
    scale_ref[...] = scales


def span_transform(table, fluid, rows_y):
    modes, points = table.shape[1:]
    width = fluid.shape[1]
    block = min(128, modes)
    return pl.pallas_call(
        functools.partial(span_kernel, rows_y, width // rows_y),
        grid=(modes // block,),
        in_specs=[
            pl.BlockSpec((2, block, points), lambda i: (0, i, 0)),
            pl.BlockSpec((points, width), lambda i: (0, 0)),
        ],
        out_specs=[
            pl.BlockSpec((block, width), lambda i: (i, 0)),
            pl.BlockSpec((block, 128), lambda i: (i, 0)),
        ],
        out_shape=[
            jax.ShapeDtypeStruct((modes, width), jnp.int16),
            jax.ShapeDtypeStruct((modes, 128), jnp.float32),
        ],
        compiler_params=pltpu.CompilerParams(vmem_limit_bytes=48 << 20),
        cost_estimate=pl.CostEstimate(
            flops=4 * modes * points * width, bytes_accessed=4 * modes * width, transcendentals=0
        ),
    )(table, fluid)


def helmholtz_kernel(
    spectra_ref, wall_ref, eigen_ref, wall_eigen_ref, into_q, into_p, from_p, from_q, out_ref
):
    spectra = spectra_ref[0]
    row = lax.broadcasted_iota(jnp.int32, spectra.shape, 0)
    spectra = spectra + jnp.where(row == 0, wall_ref[0, 0:1, :], 0.0)
    spectra = spectra + jnp.where(row == spectra.shape[0] - 1, wall_ref[0, 1:2, :], 0.0)
    coeffs = table_right(table_left(into_q, spectra), into_p)
    coeffs = coeffs / (eigen_ref[0] + wall_eigen_ref[...])
    out_ref[0] = table_left(from_q, table_right(coeffs, from_p))


def helmholtz(spectra, wall_hat, eigen, wall_eigen, tables):
    modes, n_y, n_x = spectra.shape
    whole = lambda array: pl.BlockSpec(array.shape, lambda i: (0,) * array.ndim)
    each = lambda array: pl.BlockSpec((1,) + array.shape[1:], lambda i: (i, 0, 0))
    return pl.pallas_call(
        helmholtz_kernel,
        grid=(modes,),
        in_specs=[each(spectra), each(wall_hat), each(eigen), whole(wall_eigen)]
        + [whole(table) for table in tables],
        out_specs=each(spectra),
        out_shape=jax.ShapeDtypeStruct(spectra.shape, jnp.float32),
        compiler_params=pltpu.CompilerParams(vmem_limit_bytes=48 << 20),
        cost_estimate=pl.CostEstimate(
            flops=12 * modes * n_y * n_x * (n_x + n_y),
            bytes_accessed=8 * modes * n_y * n_x,
            transcendentals=0,
        ),
    )(spectra, wall_hat, eigen, wall_eigen, *tables)


def padded(array, axis, dim, width):
    size, length = (lax.axis_size(axis), array.shape[dim])
    up = [(i, (i + 1) % size) for i in range(size)]
    down = [(j, i) for i, j in up]
    last = lax.slice_in_dim(array, length - width, length, axis=dim)
    first = lax.slice_in_dim(array, 0, width, axis=dim)
    return [lax.ppermute(last, axis, up), array, lax.ppermute(first, axis, down)]


def harmonic(first, second):
    return 2.0 * first * second / (first + second)


def conduct_step(thermal, faces, trim):
    face_x, face_y, face_z = faces
    n_x, n_y, n_z = thermal.shape[1:]
    centre = thermal[:, 1:-1, :, 1:-1]
    lo_x, lo_z = trim, trim
    cells_x = slice(lo_x + 1, lo_x + n_x - 1)
    cells_z = slice(lo_z + 1, lo_z + n_z - 1)
    fx = face_x[:, lo_x : lo_x + n_x - 1, :n_y, cells_z]
    fz = face_z[:, cells_x, :n_y, lo_z : lo_z + n_z - 1]
    fy = face_y[:, cells_x, : n_y - 1, cells_z]
    change = fx[:, 1:] * (thermal[:, 2:, :, 1:-1] - centre)
    change = change + fx[:, :-1] * (thermal[:, :-2, :, 1:-1] - centre)
    change = change + fz[..., 1:] * (thermal[:, 1:-1, :, 2:] - centre)
    change = change + fz[..., :-1] * (thermal[:, 1:-1, :, :-2] - centre)
    normal = fy * (centre[:, :, 1:] - centre[:, :, :-1])
    change = (
        change
        + jnp.pad(normal, ((0, 0), (0, 0), (0, 1), (0, 0)))
        - jnp.pad(normal, ((0, 0), (0, 0), (1, 0), (0, 0)))
    )
    return centre + SOLID_STEP * change


def per_device(fluid_temp, solid_temp, material):
    n_mode = lax.axis_size("mode")
    n_tile = lax.axis_size("tile")
    n_dev = n_mode * n_tile
    mode_idx = lax.axis_index("mode")
    tile_idx = lax.axis_index("tile")
    z_rows, y_rows, n_x = fluid_temp.shape
    n_z = z_rows * n_mode
    n_y = y_rows * n_tile
    x_rows = solid_temp.shape[1]
    z_cols = solid_temp.shape[3]
    per_dev = n_z // n_dev
    rows_y = y_rows // n_mode
    halo = SUBSTEPS

    span = fourier_table(n_z)
    span_wide = jnp.asarray(
        np.concatenate([span[:, -halo:], span, span[:, :halo]], axis=1), jnp.float32
    )
    span_wide = lax.dynamic_slice_in_dim(span_wide, tile_idx * z_cols, z_cols + 2 * halo, axis=1)
    span_own = span_wide[:, halo : halo + z_cols]

    blocks = fluid_temp.reshape(z_rows, n_mode, rows_y * n_x).transpose(1, 0, 2)
    fluid = lax.all_to_all(blocks, "mode", split_axis=0, concat_axis=0, tiled=True)
    codes, scales = span_transform(
        jnp.asarray(split_table(SIGMA * span)), fluid.reshape(n_z, rows_y * n_x), rows_y
    )

    wall_part = jnp.einsum(
        "mz,wxz->mwx", span_own, solid_temp[:, :, 0, :], precision=HIGHEST
    ).reshape(n_z, 2 * x_rows)
    small = jnp.concatenate([scales[:, :rows_y], wall_part], axis=1)
    small = lax.all_to_all(small, BOTH, split_axis=0, concat_axis=0, tiled=True)
    codes = lax.all_to_all(codes, BOTH, split_axis=0, concat_axis=0, tiled=True)
    small = small.reshape(n_mode, n_tile, per_dev, rows_y + 2 * x_rows)
    wall_hat = (
        small[..., rows_y:]
        .sum(axis=1)
        .reshape(n_mode, per_dev, 2, x_rows)
        .transpose(1, 2, 0, 3)
        .reshape(per_dev, 2, n_x)
    )
    scales = small[..., :rows_y].reshape(n_dev, per_dev, rows_y, 1)
    spectra = codes.reshape(n_dev, per_dev, rows_y, n_x).astype(jnp.float32) * scales
    spectra = spectra.transpose(1, 0, 2, 3).reshape(per_dev, n_y, n_x)

    arrived = np.arange(n_y).reshape(n_tile, n_mode, rows_y).transpose(1, 0, 2).reshape(n_y)
    sine = sine_table(n_y)
    stream = fourier_table(n_x)
    tables = [
        jnp.asarray(split_table(table)) for table in (sine[arrived].T, stream.T, stream, sine)
    ]
    span_eigen = lax.dynamic_slice_in_dim(
        jnp.asarray(fourier_eigen(n_z), jnp.float32),
        (mode_idx * n_tile + tile_idx) * per_dev,
        per_dev,
    )
    stream_eigen = jnp.asarray(fourier_eigen(n_x), jnp.float32)
    eigen = SIGMA + span_eigen[:, None, None] + stream_eigen[None, None, :]
    wall_eigen = jnp.asarray(sine_eigen(n_y), jnp.float32)[:, None]
    fluid_modes = helmholtz(spectra, wall_hat, eigen, wall_eigen, tables)

    conduct = jnp.where(
        material == 0, 0.5, jnp.where(material == 1, 1.0, jnp.where(material == 2, 2.0, 4.0))
    ).astype(jnp.float32)
    both = jnp.concatenate(padded(jnp.stack([solid_temp, conduct]), "mode", 2, halo), axis=2)
    before, both, after = padded(both, "tile", 4, halo)
    both = jnp.concatenate([before, both, after], axis=4)
    start, conduct = both[0], both[1]
    faces = (
        harmonic(conduct[:, 1:], conduct[:, :-1]),
        harmonic(conduct[:, :, 1:], conduct[:, :, :-1]),
        harmonic(conduct[..., 1:], conduct[..., :-1]),
    )
    thermal = start
    for trim in range(SUBSTEPS):
        thermal = conduct_step(thermal, faces, trim)

    near = jnp.stack([fluid_modes[:, 0, :], fluid_modes[:, n_y - 1, :]], axis=1)
    near = jnp.concatenate([near[..., -halo:], near, near[..., :halo]], axis=2)
    span_x = x_rows + 2 * halo
    near = jnp.stack([near[..., b * x_rows : b * x_rows + span_x] for b in range(n_mode)])
    near = jnp.broadcast_to(
        near.reshape(n_mode, 1, per_dev, 2 * span_x), (n_mode, n_tile, per_dev, 2 * span_x)
    ).reshape(n_z, 2 * span_x)
    near = lax.all_to_all(near, BOTH, split_axis=0, concat_axis=0, tiled=True)
    wall_flux = jnp.einsum(
        "mwx,mz->wxz", near.reshape(n_z, 2, span_x), span_wide, precision=HIGHEST
    )
    wall_flux = SOLID_STEP * (wall_flux - start[:, :, 0, :])
    added = jnp.pad(wall_flux[:, :, None, :], ((0, 0), (0, 0), (0, SUBSTEPS - 1), (0, 0)))
    source = added
    added = added[:, 1:-1, :, 1:-1]
    for trim in range(1, SUBSTEPS):
        ring = slice(trim + 1, -trim - 1)
        added = conduct_step(added, faces, trim) + source[:, ring, :, ring]
    thermal = jnp.concatenate(
        [thermal[:, :, :SUBSTEPS] + added, thermal[:, :, SUBSTEPS:]], axis=2
    )
    return (fluid_modes, thermal)


def solution(mesh):
    placed = (P("mode", "tile", None), P(None, "mode", None, "tile"), P(None, "mode", None, "tile"))
    return jax.shard_map(
        per_device,
        mesh=mesh,
        in_specs=placed,
        out_specs=(P(BOTH, None, None), P(None, "mode", None, "tile")),
        check_vma=False,
    )
```

time: 1820 us -> 761 us (0.42)
  waiting for transfers between devices: 680 us -> 61.2 us
  matrix products: 192 us -> 10.5 us
  local copies, waits for them, and re-layouts: 234 us -> 94.2 us
  other arithmetic: 601 us -> 476 us
  Pallas kernels: 0 us -> 81.2 us
  starting transfers between devices: 86.4 us -> 29.6 us
    all_to_all x3 -> x4, waiting for transfers between devices: 437 us -> 8.11 us  [the longest x1 8.1 us: per_device(): codes = lax.all_to_all(codes, BOTH, split_axis=0, concat_axis=0, tiled=True)]
    add x6 -> x9, other arithmetic: 15 us -> 260 us  [the longest x4 248 us: conduct_step(): return centre + SOLID_STEP * change]
    sub x6 -> x0, other arithmetic: 232 us -> none  [the longest x4 232 us: substep(): divergence + jnp.pad(normal, ((0, 0), (0, 0), (0, 1), (0, 0)))]
    dot_general x10 -> x2, matrix products: 192 us -> 10.5 us  [the longest x1 6.66 us: per_device(): jnp.einsum('mwx,mz->wxz', near.reshape(n_z, 2, span_x), span_wide, precis...]
    concatenate x8 -> x4, other arithmetic: 150 us -> 28.7 us  [the longest x1 26.1 us: per_device(): both = jnp.concatenate([before, both, after], axis=4)]
    reduce_scatter x1 -> x0, waiting for transfers between devices: 103 us -> none  [per_device(): lax.psum_scatter(jnp.einsum('kwmx,kmz->kwxz', columns, picked, precision=...]
    ppermute x16 -> x4, waiting for transfers between devices: 140 us -> 53.1 us  [the longest x2 37.7 us: padded(): lax.ppermute(last, axis, up)]
    pallas_call x0 -> x2, Pallas kernels: none -> 81.2 us  [the longest x1 56.5 us: helmholtz(): pl.pallas_call(helmholtz_kernel, grid=(modes,), in_specs=[each(spectra),...]
  transfers between devices with their start and end apart: 21 -> 8, of which waited for: 10 -> 4; matrix products, arithmetic and copies ran while one was open for 15% -> 63% of each run, Pallas kernels for 0% -> 0%
where the time goes in v1:
time: 761 us; the launch traced here: 754 us
  other arithmetic  476 us (63%)
  local copies, waits for them, and re-layouts  94.2 us (12%)
  Pallas kernels  81.2 us (11%)
  waiting for transfers between devices  61.2 us (8%)
  starting transfers between devices  29.6 us (4%)
  matrix products  10.5 us (1%)
    add x4, other arithmetic, conduct_step(): return centre + SOLID_STEP * change  248 us
    mul x7, other arithmetic, conduct_step(): normal = fy * (centre[:, :, 1:] - centre[:, :, :-1])  89.7 us
    pallas_call x1, Pallas kernels, helmholtz(): pl.pallas_call(helmholtz_kernel, grid=(modes,), in_specs=[each(spectra),...  56.5 us
    div x3, other arithmetic, harmonic(): return 2.0 * first * second / (first + second)  49.4 us
    ppermute x2, waiting for transfers between devices, padded(): lax.ppermute(last, axis, up)  37.7 us
    unnamed x40, local copies, waits for them, and re-layouts  33.3 us
    concatenate x1, other arithmetic, per_device(): both = jnp.concatenate([before, both, after], axis=4)  26.1 us
    pallas_call x1, Pallas kernels, span_transform(): pl.pallas_call(functools.partial(span_kernel, rows_y, width // rows_y), g...  24.8 us
  transfers between devices with their start and end apart: 8, of which 4 were waited for; matrix products, arithmetic and copies ran while one was open for 63% of the time, Pallas kernels for 0%

profile of v1, /device:TPU:1, one launch (start us, length us, event | category | flops | bytes accessed | tf_op | source)
XLA Modules:
  0.0 753.9 jit_solution(842789187689592179)
XLA Ops:
  0.6 16.5 %select_bitcast_fusion = (f32[1,2,32,64,512]{4,2,1,3,0:T(8,128)S(1)}, f32[1,2,32,64,512]{4,2,1,3,0:T(8,128)S(1)}) fusion(s32[2,32,64,512]{3,2,1,0:T(8,128)} %param.14, f32[2,32,64,512]{3,2,1,0:T(8,128)} %param.13), kind=kLoop, calls=%fused_computation.76 | loop fusion | flops 12582912 | bytes 33554432 | tf_op jit(solution)/shard_map/stack | solution.py:243
  27.6 13.4 %reshape.122 = bf16[64,16,4096]{2,1,0:T(8,128)(2,1)} reshape(bf16[64,128,512]{2,1,0:T(8,128)(2,1)} %param.12) | data formatting | bytes 16777216 | tf_op jit(solution)/shard_map/reshape | solution.py:200
  41.0 11.2 %copy.67 = bf16[64,16,4096]{2,0,1:T(8,128)(2,1)} copy(bf16[64,16,4096]{2,1,0:T(8,128)(2,1)} %reshape.122) | data formatting | bytes 16777216 | tf_op jit(solution)/shard_map/reshape | solution.py:200
  65.8 29.4 %collective-permute-done = f32[2,2,4,64,512]{4,2,1,3,0:T(4,128)S(1)} collective-permute-done((f32[2,2,4,64,512]{4,2,1,3,0:T(4,128)}, f32[2,2,4,64,512]{4,2,1,3,0:T(4,128)S(1)}, u32[]{:S(2)}, u32[]{:S(2)}) %collective-permute-start) | collective-permute-done | bytes 2097184 | tf_op jit(solution)/shard_map/ppermute | solution.py:148
  95.3 15.5 %collective-permute-done.1 = f32[2,2,4,64,512]{4,2,1,3,0:T(4,128)} collective-permute-done((f32[2,2,4,64,512]{4,2,1,3,0:T(4,128)}, f32[2,2,4,64,512]{4,2,1,3,0:T(4,128)}, u32[]{:S(2)}, u32[]{:S(2)}) %collective-permute-start.1) | collective-permute-done | bytes 2097184 | tf_op jit(solution)/shard_map/ppermute | solution.py:148
  110.7 8.3 %pad_maximum_fusion.5 = (f32[2,2,40,64,4]{4,2,1,3,0:T(8,128)}, f32[2,2,40,64,4]{4,2,1,3,0:T(8,128)}) fusion(f32[2,2,4,64,512]{4,2,1,3,0:T(4,128)} %collective-permute-done.1, f32[2,2,4,64,512]{4,2,1,3,0:T(4,128)S(1)} %collective-permute-done, f32[1,2,32,64,512]{4,2,1,3,0:T(8,128)} %copy-done.7, f32[1,2,32,64,512]{4,2,1,3,0:T(8,128)} %copy-done.8), kind=kLoop, calls=%fused_computation.82 | loop fusion | flops 245760 | bytes 21299200 | tf_op jit(solution)/shard_map/slice | solution.py:146
  143.4 26.1 %pad_maximum_fusion = f32[2,2,40,64,520]{4,2,1,3,0:T(8,128)} fusion(f32[2,2,40,64,4]{4,2,1,3,0:T(8,128)} %copy.51, f32[2,2,4,64,512]{4,2,1,3,0:T(4,128)} %collective-permute-done.1, f32[1,2,32,64,512]{4,2,1,3,0:T(8,128)} %copy-done.7, f32[1,2,32,64,512]{4,2,1,3,0:T(8,128)} %copy-done.8, f32[2,2,4,64,512]{4,2,1,3,0:T(4,128)S(1)} %collective-permute-done, ...), kind=kLoop, calls=%fused_computation | loop fusion | flops 26624000 | bytes 42598400 | tf_op jit(solution)/shard_map/concatenate | solution.py:245
  169.5 13.9 %slice_bitcast_fusion = (f32[2,40,64,520]{3,1,0,2:T(8,128)}, f32[2,40,64,520]{3,1,0,2:T(8,128)S(1)}) fusion(f32[2,2,40,64,520]{4,2,1,3,0:T(8,128)} %pad_maximum_fusion), kind=kLoop, calls=%fused_computation.48 | loop fusion | bytes 42598400 | tf_op jit(solution)/shard_map/squeeze | solution.py:246
  183.5 19.1 %add_divide_fusion.2 = f32[2,40,63,520]{3,1,0,2:T(8,128)} fusion(f32[2,40,64,520]{3,1,0,2:T(8,128)} %get-tuple-element.12), kind=kLoop, calls=%fused_computation.58 | loop fusion | flops 10483200 | bytes 31449600 | tf_op jit(solution)/shard_map/div | solution.py:152
  202.6 18.8 %fusion.36 = f32[2,38,63,518]{3,1,0,2:T(8,128)} fusion(f32[2,40,64,520]{3,1,0,2:T(8,128)S(1)} %get-tuple-element.13, f32[2,40,63,520]{3,1,0,2:T(8,128)} %add_divide_fusion.2), kind=kLoop, calls=%fused_computation.57 | loop fusion | flops 4960368 | bytes 39682944 | tf_op jit(solution)/shard_map/mul | solution.py:169
  221.4 15.2 %add_divide_fusion = f32[2,40,64,519]{3,1,0,2:T(8,128)} fusion(f32[2,40,64,520]{3,1,0,2:T(8,128)} %get-tuple-element.12), kind=kLoop, calls=%fused_computation.50 | loop fusion | flops 10629120 | bytes 31887360 | tf_op jit(solution)/shard_map/div | solution.py:152
  236.6 15.1 %add_divide_fusion.1 = f32[2,39,64,520]{3,1,0,2:T(8,128)} fusion(f32[2,40,64,520]{3,1,0,2:T(8,128)} %get-tuple-element.12), kind=kLoop, calls=%fused_computation.51 | loop fusion | flops 10383360 | bytes 31150080 | tf_op jit(solution)/shard_map/div | solution.py:152
  251.7 63.5 %fusion.28 = f32[2,38,64,518]{3,1,0,2:T(8,128)} fusion(f32[2,40,64,520]{3,1,0,2:T(8,128)} %copy-done.6, f32[2,40,64,519]{3,1,0,2:T(8,128)} %add_divide_fusion, f32[2,39,64,520]{3,1,0,2:T(8,128)} %add_divide_fusion.1, f32[2,38,63,518]{3,1,0,2:T(8,128)} %fusion.36), kind=kLoop, calls=%fused_computation.39 | loop fusion | flops 37793280 | bytes 110702816 | tf_op jit(solution)/shard_map/add | solution.py:175
  317.4 24.8 %shard_map.131 = (s16[1024,4096]{1,0:T(8,128)(2,1)}, f32[1024,128]{1,0:T(8,128)S(1)}) custom-call(bf16[2,1024,1024]{2,1,0:T(8,128)(2,1)S(1)} %copy-done, bf16[1024,4096]{1,0:T(8,128)(2,1)} %bitcast.1.fluid_ref), custom_call_target="tpu_custom_call" | custom-call | flops 17179869184 | bytes 16777216 | tf_op jit(solution)/shard_map/pallas_call | solution.py:88
  346.6 23.6 %fusion.35 = f32[2,36,63,516]{3,1,0,2:T(8,128)} fusion(f32[2,38,64,518]{3,1,0,2:T(8,128)} %fusion.28, f32[2,40,63,520]{3,1,0,2:T(8,128)} %add_divide_fusion.2), kind=kLoop, calls=%fused_computation.55 | loop fusion | flops 4681152 | bytes 37449216 | tf_op jit(solution)/shard_map/mul | solution.py:169
  376.4 64.4 %fusion.17 = f32[2,36,64,516]{3,1,0,2:T(8,128)} fusion(f32[2,38,64,518]{3,1,0,2:T(8,128)} %fusion.28, f32[2,40,64,519]{3,1,0,2:T(8,128)} %add_divide_fusion, f32[2,39,64,520]{3,1,0,2:T(8,128)} %add_divide_fusion.1, f32[2,36,63,516]{3,1,0,2:T(8,128)} %fusion.35), kind=kLoop, calls=%fused_computation.24 | loop fusion | flops 35665920 | bytes 104471424 | tf_op jit(solution)/shard_map/add | solution.py:175
  440.8 23.5 %fusion.34 = f32[2,34,63,514]{3,1,0,2:T(8,128)} fusion(f32[2,36,64,516]{3,1,0,2:T(8,128)} %fusion.17, f32[2,40,63,520]{3,1,0,2:T(8,128)} %add_divide_fusion.2), kind=kLoop, calls=%fused_computation.53 | loop fusion | flops 4403952 | bytes 35231616 | tf_op jit(solution)/shard_map/mul | solution.py:169
  464.2 66.8 %fusion.6 = f32[2,34,64,514]{3,1,0,2:T(8,128)} fusion(f32[2,36,64,516]{3,1,0,2:T(8,128)} %fusion.17, f32[2,40,64,519]{3,1,0,2:T(8,128)} %add_divide_fusion, f32[2,39,64,520]{3,1,0,2:T(8,128)} %add_divide_fusion.1, f32[2,34,63,514]{3,1,0,2:T(8,128)} %fusion.34), kind=kLoop, calls=%fused_computation.9 | loop fusion | flops 33553920 | bytes 98285024 | tf_op jit(solution)/shard_map/add | solution.py:175
  531.1 19.2 %fusion.48 = f32[2,32,63,512]{3,1,0,2:T(8,128)} fusion(f32[2,34,64,514]{3,1,0,2:T(8,128)} %fusion.6, f32[2,40,63,520]{3,1,0,2:T(8,128)} %add_divide_fusion.2), kind=kLoop, calls=%fused_computation.78 | loop fusion | flops 4128768 | bytes 33030144 | tf_op jit(solution)/shard_map/mul | solution.py:169
  559.8 12.4 %convert.1 = f32[128,8,8,512]{3,1,2,0:T(8,128)} convert(s16[128,8,8,512]{3,1,2,0:T(8,128)(2,1)} %bitcast.43) | non-fusion elementwise | flops 4194304 | bytes 25165824
  572.2 19.1 %copy.55 = f32[128,8,8,512]{3,2,1,0:T(8,128)S(1)} copy(f32[128,8,8,512]{3,1,2,0:T(8,128)} %convert.1) | data formatting | bytes 33554432
  597.7 56.5 %shard_map.132 = f32[32,256,512]{2,1,0:T(8,128)} custom-call(f32[32,256,512]{2,1,0:T(8,128)} %fusion.spectra_ref, f32[32,2,512]{2,1,0:T(2,128)S(1)} %reshape.127.wall_ref, f32[32,1,512]{2,1,0:T(1,128)S(1)} %broadcast_add_fusion.eigen_ref, f32[256,1]{1,0:T(8,128)S(1)} %copy-done.5, bf16[2,256,256]{2,1,0:T(8,128)(2,1)S(1)} %copy-done.4, ...), custom_call_target="tpu_custom_call" | custom-call | flops 38654705664 | bytes 33554432 | tf_op jit(solution)/shard_map/pallas_call | solution.py:126
  667.2 53.1 %fusion.42 = f32[2,32,64,512]{3,1,0,2:T(8,128)} fusion(f32[2,34,64,514]{3,1,0,2:T(8,128)} %fusion.6, f32[2,40,64,519]{3,1,0,2:T(8,128)} %add_divide_fusion, f32[2,39,64,520]{3,1,0,2:T(8,128)} %add_divide_fusion.1, f32[2,32,63,512]{3,1,0,2:T(8,128)} %fusion.48), kind=kLoop, calls=%fused_computation.65 | loop fusion | flops 31457280 | bytes 92143616 | tf_op jit(solution)/shard_map/add | solution.py:175
  745.2 8.5 %copy.53 = f32[2,32,64,512]{3,2,1,0:T(8,128)} copy(f32[2,32,64,512]{3,1,0,2:T(8,128)S(1)} %pad_maximum_fusion.1) | data formatting | bytes 16777216
  (103 shorter events, 114.6 us)
Async XLA Ops:
  17.1 3.4 copy-start.7
  17.1 7.3 copy-start.8
  24.4 70.9 %collective-permute-start = (f32[2,2,4,64,512]{4,2,1,3,0:T(4,128)}, f32[2,2,4,64,512]{4,2,1,3,0:T(4,128)S(1)}, u32[]{:S(2)}, u32[]{:S(2)}) collective-permute-start(f32[2,2,4,64,512]{4,2,1,3,0:T(4,128)} %get-tuple-element.18), channel_id=1, source_target_pairs={{0,2},{2,4},{4,6},{6,8},{8,10},{10,12},{12,14},{14,16},{16,18},{18... | collective-permute-start | bytes 6291464 | tf_op jit(solution)/shard_map/ppermute | solution.py:148
  27.0 83.7 %collective-permute-start.1 = (f32[2,2,4,64,512]{4,2,1,3,0:T(4,128)}, f32[2,2,4,64,512]{4,2,1,3,0:T(4,128)}, u32[]{:S(2)}, u32[]{:S(2)}) collective-permute-start(f32[2,2,4,64,512]{4,2,1,3,0:T(4,128)} %get-tuple-element.19), channel_id=1, source_target_pairs={{2,0},{4,2},{6,4},{8,6},{10,8},{12,10},{14,12},{16,14},{18,16},{20... | collective-permute-start | bytes 6291464 | tf_op jit(solution)/shard_map/ppermute | solution.py:148
  52.2 263.1 %all-to-all-start = ((bf16[16,64,4096]{2,1,0:T(8,128)(2,1)}), bf16[16,64,4096]{2,1,0:T(8,128)(2,1)}, u32[]{:S(2)}, u32[]{:S(2)}) async-start(bf16[16,64,4096]{2,1,0:T(8,128)(2,1)} %bitcast.55), calls=%async_computation | async-start | bytes 16777216 | tf_op jit(solution)/shard_map/all_to_all | solution.py:201
  65.8 62.1 %copy-start.10 = (f32[512]{0:T(512)S(1)}, f32[512]{0:T(512)}, u32[]{:S(2)}) copy-start(f32[512]{0:T(512)} %constant.23.clone) | copy-start | bytes 6148
  126.5 13.4 %collective-permute-start.3 = (f32[2,2,40,64,4]{3,2,4,1,0:T(8,128)S(1)}, f32[2,2,40,64,4]{3,2,4,1,0:T(8,128)S(1)}, u32[]{:S(2)}, u32[]{:S(2)}) collective-permute-start(f32[2,2,40,64,4]{3,2,4,1,0:T(8,128)S(1)} %copy.49), channel_id=1, source_target_pairs={{1,0},{0,1},{3,2},{2,3},{5,4},{4,5},{7,6},{6,7},{9,8},{8,9},{11,10... | collective-permute-start | bytes 491528 | tf_op jit(solution)/shard_map/ppermute | solution.py:148
  127.8 8.6 %collective-permute-start.2 = (f32[2,2,40,64,4]{3,2,4,1,0:T(8,128)S(1)}, f32[2,2,40,64,4]{3,2,4,1,0:T(8,128)S(1)}, u32[]{:S(2)}, u32[]{:S(2)}) collective-permute-start(f32[2,2,40,64,4]{3,2,4,1,0:T(8,128)S(1)} %copy.48), channel_id=1, source_target_pairs={{0,1},{1,0},{2,3},{3,2},{4,5},{5,4},{6,7},{7,6},{8,9},{9,8},{10,11... | collective-permute-start | bytes 491528 | tf_op jit(solution)/shard_map/ppermute | solution.py:148
  183.5 19.1 %copy-start.6 = (f32[2,40,64,520]{3,1,0,2:T(8,128)}, f32[2,40,64,520]{3,1,0,2:T(8,128)S(1)}, u32[]{:S(2)}) copy-start(f32[2,40,64,520]{3,1,0,2:T(8,128)S(1)} %get-tuple-element.13) | copy-start | bytes 31948804
  315.2 2.2 copy-start
  317.4 24.9 %copy-start.9 = (f32[1024,64]{0,1:T(8,128)S(1)}, f32[1024,64]{0,1:T(8,128)}, u32[]{:S(2)}) copy-start(f32[1024,64]{0,1:T(8,128)} %fusion.52) | copy-start | bytes 786436
  343.4 26.7 %all-to-all-start.2 = ((f32[32,32,72]{2,1,0:T(8,128)}), f32[32,32,72]{2,1,0:T(8,128)S(1)}, u32[]{:S(2)}, u32[]{:S(2)}) async-start(f32[32,32,72]{2,1,0:T(8,128)} %bitcast.4), calls=%async_computation.2 | async-start | bytes 1048576 | tf_op jit(solution)/shard_map/all_to_all | solution.py:210
  370.2 189.6 %all-to-all-start.1 = ((s16[32,32,4096]{2,1,0:T(8,128)(2,1)}), s16[32,32,4096]{2,1,0:T(8,128)(2,1)}, u32[]{:S(2)}, u32[]{:S(2)}) async-start(s16[32,32,4096]{2,1,0:T(8,128)(2,1)} %bitcast.56), calls=%async_computation.1 | async-start | bytes 16777216 | tf_op jit(solution)/shard_map/all_to_all | solution.py:211
  591.4 6.3 copy-start.1
  591.4 6.3 copy-start.2
  591.4 6.3 copy-start.3
  591.4 6.3 copy-start.4
  591.4 6.3 copy-start.5
  659.4 60.9 %all-to-all-start.3 = ((f32[32,32,80]{2,1,0:T(8,128)}), f32[32,32,80]{2,1,0:T(8,128)S(1)}, u32[]{:S(2)}, u32[]{:S(2)}) async-start(f32[32,32,80]{2,1,0:T(8,128)} %bitcast.15), calls=%async_computation.3 | async-start | bytes 1048576 | tf_op jit(solution)/shard_map/all_to_all | solution.py:263
  727.6 15.7 %slice-start = ((f32[2,32,64,512]{3,1,0,2:T(8,128)}), f32[2,32,60,512]{3,1,0,2:T(8,128)S(1)}, s32[]{:S(2)}) async-start(f32[2,32,64,512]{3,1,0,2:T(8,128)} %fusion.42), calls=%async_computation.4 | async-start | bytes 15728640 | tf_op jit(solution)/shard_map/slice | solution.py:275

commit v2 on v1

--- a/solution.py
+++ b/solution.py
@@ -175,6 +175,63 @@
     return centre + SOLID_STEP * change
 
 
+def conduct_kernel(thermal_ref, conduct_ref, out_ref, held, face_x, face_y, face_z):
+    planes, n_y, n_z = held.shape
+    n_out = out_ref.shape[3]
+    row = lax.broadcasted_iota(jnp.int32, (n_y, n_z), 0)
+
+    def set_faces(x, carry):
+        cond = conduct_ref[0, x]
+        face_z[x] = SOLID_STEP * harmonic(pltpu.roll(cond, n_z - 1, 1), cond)
+        normal = SOLID_STEP * harmonic(pltpu.roll(cond, n_y - 1, 0), cond)
+        face_y[x] = jnp.where(row == n_y - 1, 0.0, normal)
+        ahead = conduct_ref[0, jnp.minimum(x + 1, planes - 1)]
+        face_x[x] = SOLID_STEP * harmonic(ahead, cond)
+        return carry
+
+    lax.fori_loop(0, planes, set_faces, 0)
+    for step in range(1, SUBSTEPS + 1):
+        old = thermal_ref.at[0] if step == 1 else held
+
+        def plane(x, behind):
+            here = old[x]
+            ahead = face_x[x] * (old[x + 1] - here)
+            span = face_z[x] * (pltpu.roll(here, n_z - 1, 1) - here)
+            normal = face_y[x] * (pltpu.roll(here, n_y - 1, 0) - here)
+            change = (ahead - behind) + (span - pltpu.roll(span, 1, 1))
+            change = change + (normal - pltpu.roll(normal, 1, 0))
+            if step == SUBSTEPS:
+                out_ref[0, x - SUBSTEPS] = (here + change)[:, :n_out]
+            else:
+                held[x] = here + change
+            return ahead
+
+        first = face_x[step - 1] * (old[step] - old[step - 1])
+        lax.fori_loop(step, planes - step, plane, first)
+
+
+def conduct_walls(thermal, conduct, z_cols):
+    walls, planes, n_y, n_z = thermal.shape
+    rows = planes - 2 * SUBSTEPS
+    block = pl.BlockSpec(
+        (1, planes, n_y, n_z), lambda w: (w, 0, 0, 0), pipeline_mode=pl.Buffered(1)
+    )
+    return pl.pallas_call(
+        conduct_kernel,
+        grid=(walls,),
+        in_specs=[block, block],
+        out_specs=pl.BlockSpec(
+            (1, rows, n_y, z_cols), lambda w: (w, 0, 0, 0), pipeline_mode=pl.Buffered(1)
+        ),
+        out_shape=jax.ShapeDtypeStruct((walls, rows, n_y, z_cols), jnp.float32),
+        scratch_shapes=[pltpu.VMEM((planes, n_y, n_z), jnp.float32) for _ in range(4)],
+        compiler_params=pltpu.CompilerParams(vmem_limit_bytes=54 << 20),
+        cost_estimate=pl.CostEstimate(
+            flops=80 * thermal.size * SUBSTEPS, bytes_accessed=12 * thermal.size, transcendentals=0
+        ),
+    )(thermal, conduct)
+
+
 def per_device(fluid_temp, solid_temp, material):
     n_mode = lax.axis_size("mode")
     n_tile = lax.axis_size("tile")
@@ -242,16 +299,17 @@
     ).astype(jnp.float32)
     both = jnp.concatenate(padded(jnp.stack([solid_temp, conduct]), "mode", 2, halo), axis=2)
     before, both, after = padded(both, "tile", 4, halo)
-    both = jnp.concatenate([before, both, after], axis=4)
-    start, conduct = both[0], both[1]
+    filling = jnp.ones(both.shape[:4] + (128 - 2 * halo,), jnp.float32)
+    both = jnp.concatenate([both, after, filling, before], axis=4)
+    thermal = conduct_walls(both[0], both[1], z_cols)
+    slab = both[:, :, :, :SUBSTEPS]
+    slab = jnp.concatenate([slab[..., -halo:], slab[..., : z_cols + halo]], axis=4)
+    start, conduct = slab[0], slab[1]
     faces = (
         harmonic(conduct[:, 1:], conduct[:, :-1]),
         harmonic(conduct[:, :, 1:], conduct[:, :, :-1]),
         harmonic(conduct[..., 1:], conduct[..., :-1]),
     )
-    thermal = start
-    for trim in range(SUBSTEPS):
-        thermal = conduct_step(thermal, faces, trim)
 
     near = jnp.stack([fluid_modes[:, 0, :], fluid_modes[:, n_y - 1, :]], axis=1)
     near = jnp.concatenate([near[..., -halo:], near, near[..., :halo]], axis=2)

time: 761 us -> 785 us (1.032)
  other arithmetic: 476 us -> 75.9 us
  waiting for transfers between devices: 61.2 us -> 271 us
  Pallas kernels: 81.2 us -> 164 us
  starting transfers between devices: 29.6 us -> 110 us
  blocking collectives: 0 us -> 51.6 us
    add x4 -> x0, other arithmetic: 248 us -> none  [conduct_step(): return centre + SOLID_STEP * change]
    all_to_all x1, waiting for transfers between devices: 0.01 us -> 147 us  [per_device(): lax.all_to_all(blocks, 'mode', split_axis=0, concat_axis=0, tiled=True)]
    all_to_all x1, starting transfers between devices: 7.85 us -> 96.1 us  [per_device(): near = lax.all_to_all(near, BOTH, split_axis=0, concat_axis=0, tiled=True)]
    mul x7 -> x3, other arithmetic: 89.7 us -> 2.86 us  [conduct_step(): normal = fy * (centre[:, :, 1:] - centre[:, :, :-1])]
    pallas_call x0 -> x1, Pallas kernels: none -> 83.4 us  [conduct_walls(): pl.pallas_call(conduct_kernel, grid=(walls,), in_specs=[block, block], ou...]
    ppermute x2, waiting for transfers between devices: 37.7 us -> 109 us  [padded(): lax.ppermute(last, axis, up)]
    all_to_all x0 -> x1, blocking collectives: none -> 51.6 us  [per_device(): small = lax.all_to_all(small, BOTH, split_axis=0, concat_axis=0, tiled=True)]
    div x3, other arithmetic: 49.4 us -> 1.14 us  [harmonic(): return 2.0 * first * second / (first + second)]
  transfers between devices with their start and end apart: 8 -> 7, of which waited for: 4 -> 5; matrix products, arithmetic and copies ran while one was open for 63% -> 10% of each run, Pallas kernels for 0% -> 11%
where the time goes in v2:
time: 785 us; the launch traced here: 776 us
  waiting for transfers between devices  271 us (35%)
  Pallas kernels  164 us (21%)
  starting transfers between devices  110 us (14%)
  local copies, waits for them, and re-layouts  91.7 us (12%)
  other arithmetic  75.9 us (10%)
  blocking collectives  51.6 us (7%)
  matrix products  10.1 us (1%)
    all_to_all x1, waiting for transfers between devices, per_device(): lax.all_to_all(blocks, 'mode', split_axis=0, concat_axis=0, tiled=True)  147 us
    ppermute x2, waiting for transfers between devices, padded(): lax.ppermute(last, axis, up)  109 us
    all_to_all x1, starting transfers between devices, per_device(): near = lax.all_to_all(near, BOTH, split_axis=0, concat_axis=0, tiled=True)  96.1 us
    pallas_call x1, Pallas kernels, conduct_walls(): pl.pallas_call(conduct_kernel, grid=(walls,), in_specs=[block, block], ou...  83.4 us
    pallas_call x1, Pallas kernels, helmholtz(): pl.pallas_call(helmholtz_kernel, grid=(modes,), in_specs=[each(spectra),...  56.6 us
    all_to_all x1, blocking collectives, per_device(): small = lax.all_to_all(small, BOTH, split_axis=0, concat_axis=0, tiled=True)  51.6 us
    reshape x2, local copies, waits for them, and re-layouts, per_device(): blocks = fluid_temp.reshape(z_rows, n_mode, rows_y * n_x).transpose(1, 0, 2)  24.8 us
    pallas_call x1, Pallas kernels, span_transform(): pl.pallas_call(functools.partial(span_kernel, rows_y, width // rows_y), g...  24.4 us
  transfers between devices with their start and end apart: 7, of which 5 were waited for; matrix products, arithmetic and copies ran while one was open for 10% of the time, Pallas kernels for 11%

profile of v2, /device:TPU:1, one launch (start us, length us, event | category | flops | bytes accessed | tf_op | source)
XLA Modules:
  0.0 776.0 jit_solution(2234425961236448433)
XLA Ops:
  0.6 13.4 %reshape.122 = bf16[64,16,4096]{2,1,0:T(8,128)(2,1)} reshape(bf16[64,128,512]{2,1,0:T(8,128)(2,1)} %param.12) | data formatting | bytes 16777216 | tf_op jit(solution)/shard_map/reshape | solution.py:257
  14.1 11.4 %copy.55 = bf16[64,16,4096]{2,0,1:T(8,128)(2,1)} copy(bf16[64,16,4096]{2,1,0:T(8,128)(2,1)} %reshape.122) | data formatting | bytes 16777216 | tf_op jit(solution)/shard_map/reshape | solution.py:257
  25.4 7.3 all-to-all-start
  37.3 146.6 %all-to-all-done = bf16[16,64,4096]{2,1,0:T(8,128)(2,1)} async-done(((bf16[16,64,4096]{2,1,0:T(8,128)(2,1)}), bf16[16,64,4096]{2,1,0:T(8,128)(2,1)}, u32[]{:S(2)}, u32[]{:S(2)}) %all-to-all-start) | async-done | bytes 8388640 | tf_op jit(solution)/shard_map/all_to_all | solution.py:258
  186.1 24.4 %shard_map.131 = (s16[1024,4096]{1,0:T(8,128)(2,1)}, f32[1024,128]{1,0:T(8,128)S(1)}) custom-call(bf16[2,1024,1024]{2,1,0:T(8,128)(2,1)S(1)} %copy-done, bf16[1024,4096]{1,0:T(8,128)(2,1)} %bitcast.1.fluid_ref), custom_call_target="tpu_custom_call" | custom-call | flops 17179869184 | bytes 16777216 | tf_op jit(solution)/shard_map/pallas_call | solution.py:88
  210.8 51.6 %all_to_all.32 = f32[32,32,72]{2,1,0:T(8,128)} all-to-all(f32[32,32,72]{2,1,0:T(8,128)S(1)} %bitcast.65), channel_id=1, replica_groups=mesh['mode'=16,'tile'=2] {'mode','tile'}, dimensions={0} | all-to-all | bytes 589824 | tf_op jit(solution)/shard_map/all_to_all | solution.py:267
  265.9 4.5 select_bitcast_fusion
  270.4 5.7 pad_maximum_fusion.7
  278.3 104.8 %collective-permute-done = f32[2,2,4,64,512]{4,3,2,1,0:T(8,128)S(1)} collective-permute-done((f32[2,2,4,64,512]{4,3,2,1,0:T(8,128)}, f32[2,2,4,64,512]{4,3,2,1,0:T(8,128)S(1)}, u32[]{:S(2)}, u32[]{:S(2)}) %collective-permute-start) | collective-permute-done | bytes 2097184 | tf_op jit(solution)/shard_map/ppermute | solution.py:148
  383.1 7.9 %pad_maximum_fusion.5 = (f32[2,2,40,64,4]{4,3,2,1,0:T(8,128)}, f32[2,2,40,64,4]{4,3,2,1,0:T(8,128)}) fusion(f32[2,2,4,64,512]{4,3,2,1,0:T(8,128)} %collective-permute-done.1, f32[2,2,4,64,512]{4,3,2,1,0:T(8,128)S(1)} %collective-permute-done, f32[1,2,32,64,512]{4,3,2,1,0:T(8,128)} %copy-done.6, f32[1,2,32,64,512]{4,3,2,1,0:T(8,128)} %bitcast.55), kind=kLoop, calls=%fused_computation.11 | loop fusion | flops 245760 | bytes 21299200 | tf_op jit(solution)/shard_map/slice | solution.py:147
  399.6 4.5 collective-permute-done.3
  404.1 4.2 copy.39
  417.0 13.7 %pad_maximum_fusion = f32[2,2,40,64,640]{4,3,2,1,0:T(8,128)S(1)} fusion(f32[2,2,40,64,4]{4,3,2,1,0:T(8,128)} %copy.39, f32[2,2,40,64,4]{4,3,2,1,0:T(8,128)} %copy.38, f32[2,2,4,64,512]{4,3,2,1,0:T(8,128)} %collective-permute-done.1, f32[1,2,32,64,512]{4,3,2,1,0:T(8,128)} %copy-done.6, f32[1,2,32,64,512]{4,3,2,1,0:T(8,128)} %bitcast.57, ...), kind=kLoop, calls=%fused_computation | loop fusion | flops 39321600 | bytes 47516160 | tf_op jit(solution)/shard_map/concatenate | solution.py:303
  430.7 9.3 %slice_bitcast_fusion = (f32[2,40,64,640]{3,2,1,0:T(8,128)}, f32[2,40,64,640]{3,2,1,0:T(8,128)}) fusion(f32[2,2,40,64,640]{4,3,2,1,0:T(8,128)S(1)} %pad_maximum_fusion), kind=kLoop, calls=%fused_computation.3 | loop fusion | bytes 52428800 | tf_op jit(solution)/shard_map/squeeze | solution.py:304
  440.1 83.4 %shard_map.133 = f32[2,32,64,512]{3,2,1,0:T(8,128)} custom-call(f32[2,40,64,640]{3,2,1,0:T(8,128)} %get-tuple-element.7.thermal_ref, f32[2,40,64,640]{3,2,1,0:T(8,128)} %get-tuple-element.6.conduct_ref), custom_call_target="tpu_custom_call" | custom-call | flops 1048576000 | bytes 39321600 | tf_op jit(solution)/shard_map/pallas_call | solution.py:219
  523.4 8.2 %slice.442 = f32[2,32,60,512]{3,2,1,0:T(8,128)} slice(f32[2,32,64,512]{3,2,1,0:T(8,128)} %shard_map.133), slice={[0:2], [0:32], [4:64], [0:512]} | slice | bytes 15728640 | tf_op jit(solution)/shard_map/slice | solution.py:333
  535.4 12.4 %convert.1 = f32[128,8,8,512]{3,1,2,0:T(8,128)} convert(s16[128,8,8,512]{3,1,2,0:T(8,128)(2,1)} %bitcast.42) | non-fusion elementwise | flops 4194304 | bytes 25165824
  547.9 19.1 %copy.47 = f32[128,8,8,512]{3,2,1,0:T(8,128)S(1)} copy(f32[128,8,8,512]{3,1,2,0:T(8,128)} %convert.1) | data formatting | bytes 33554432
  567.1 6.1 fusion.spectra_ref
  573.3 56.6 %shard_map.132 = f32[32,256,512]{2,1,0:T(8,128)} custom-call(f32[32,256,512]{2,1,0:T(8,128)} %fusion.spectra_ref, f32[32,2,512]{2,1,0:T(2,128)S(1)} %reshape.127.wall_ref, f32[32,1,512]{2,1,0:T(1,128)S(1)} %broadcast_add_fusion.eigen_ref, f32[256,1]{1,0:T(8,128)S(1)} %copy-done.5, bf16[2,256,256]{2,1,0:T(8,128)(2,1)S(1)} %copy-done.4, ...), custom_call_target="tpu_custom_call" | custom-call | flops 38654705664 | bytes 33554432 | tf_op jit(solution)/shard_map/pallas_call | solution.py:126
  635.1 96.1 %all-to-all-start.3 = ((f32[32,32,80]{2,1,0:T(8,128)}), f32[32,32,80]{2,1,0:T(8,128)}, u32[]{:S(2)}, u32[]{:S(2)}) async-start(f32[32,32,80]{2,1,0:T(8,128)} %bitcast.15), calls=%async_computation.3 | async-start | bytes 1048576 | tf_op jit(solution)/shard_map/all_to_all | solution.py:321
  731.9 15.2 %all-to-all-done.3 = f32[32,32,80]{2,1,0:T(8,128)} async-done(((f32[32,32,80]{2,1,0:T(8,128)}), f32[32,32,80]{2,1,0:T(8,128)}, u32[]{:S(2)}, u32[]{:S(2)}) %all-to-all-start.3) | async-done | bytes 327712 | tf_op jit(solution)/shard_map/all_to_all | solution.py:321
  749.7 6.9 fusion.10
  771.1 4.7 pad_maximum_fusion.1
  (101 shorter events, 56.4 us)
Async XLA Ops:
  25.4 158.5 %all-to-all-start = ((bf16[16,64,4096]{2,1,0:T(8,128)(2,1)}), bf16[16,64,4096]{2,1,0:T(8,128)(2,1)}, u32[]{:S(2)}, u32[]{:S(2)}) async-start(bf16[16,64,4096]{2,1,0:T(8,128)(2,1)} %bitcast.61), calls=%async_computation | async-start | bytes 16777216 | tf_op jit(solution)/shard_map/all_to_all | solution.py:258
  183.9 2.2 copy-start
  262.4 273.0 %all-to-all-start.1 = ((s16[32,32,4096]{2,1,0:T(8,128)(2,1)}), s16[32,32,4096]{2,1,0:T(8,128)(2,1)}, u32[]{:S(2)}, u32[]{:S(2)}) async-start(s16[32,32,4096]{2,1,0:T(8,128)(2,1)} %bitcast.62), calls=%async_computation.1 | async-start | bytes 16777216 | tf_op jit(solution)/shard_map/all_to_all | solution.py:268
  270.4 5.7 copy-start.6
  276.1 107.0 %collective-permute-start = (f32[2,2,4,64,512]{4,3,2,1,0:T(8,128)}, f32[2,2,4,64,512]{4,3,2,1,0:T(8,128)S(1)}, u32[]{:S(2)}, u32[]{:S(2)}) collective-permute-start(f32[2,2,4,64,512]{4,3,2,1,0:T(8,128)} %get-tuple-element.12), channel_id=1, source_target_pairs={{0,2},{2,4},{4,6},{6,8},{8,10},{10,12},{12,14},{14,16},{16,18},{18... | collective-permute-start | bytes 6291464 | tf_op jit(solution)/shard_map/ppermute | solution.py:148
  277.2 106.0 %collective-permute-start.1 = (f32[2,2,4,64,512]{4,3,2,1,0:T(8,128)}, f32[2,2,4,64,512]{4,3,2,1,0:T(8,128)}, u32[]{:S(2)}, u32[]{:S(2)}) collective-permute-start(f32[2,2,4,64,512]{4,3,2,1,0:T(8,128)} %get-tuple-element.13), channel_id=1, source_target_pairs={{2,0},{4,2},{6,4},{8,6},{10,8},{12,10},{14,12},{16,14},{18,16},{20... | collective-permute-start | bytes 6291464 | tf_op jit(solution)/shard_map/ppermute | solution.py:148
  391.1 8.5 %copy-start.8 = (f32[512]{0:T(512)S(1)}, f32[512]{0:T(512)}, u32[]{:S(2)}) copy-start(f32[512]{0:T(512)} %constant.71.clone) | copy-start | bytes 6148
  398.0 6.1 collective-permute-start.3
  398.1 11.4 %collective-permute-start.2 = (f32[2,2,40,64,4]{3,2,4,1,0:T(8,128)S(1)}, f32[2,2,40,64,4]{3,2,4,1,0:T(8,128)S(1)}, u32[]{:S(2)}, u32[]{:S(2)}) collective-permute-start(f32[2,2,40,64,4]{3,2,4,1,0:T(8,128)S(1)} %copy.36), channel_id=1, source_target_pairs={{1,0},{0,1},{3,2},{2,3},{5,4},{4,5},{7,6},{6,7},{9,8},{8,9},{11,10... | collective-permute-start | bytes 491528 | tf_op jit(solution)/shard_map/ppermute | solution.py:148
  523.4 8.8 %copy-start.7 = (f32[32,32,72]{2,1,0:T(8,128)S(1)}, f32[32,32,72]{2,1,0:T(8,128)}, u32[]{:S(2)}) copy-start(f32[32,32,72]{2,1,0:T(8,128)} %all_to_all.32) | copy-start | bytes 884740
  567.0 6.2 copy-start.1
  567.0 6.2 copy-start.2
  567.0 6.2 copy-start.3
  567.1 6.2 copy-start.4
  567.1 6.2 copy-start.5
  635.1 112.0 %all-to-all-start.3 = ((f32[32,32,80]{2,1,0:T(8,128)}), f32[32,32,80]{2,1,0:T(8,128)}, u32[]{:S(2)}, u32[]{:S(2)}) async-start(f32[32,32,80]{2,1,0:T(8,128)} %bitcast.15), calls=%async_computation.3 | async-start | bytes 1048576 | tf_op jit(solution)/shard_map/all_to_all | solution.py:321
  762.4 8.7 %slice-start = ((s8[8388608]{0:T(1024)(128)(4,1)}), s8[4194304]{0:T(1024)(128)(4,1)S(1)}, s32[]{:S(2)}) async-start(s8[8388608]{0:T(1024)(128)(4,1)} %bitcast.59), calls=%async_computation.4 | async-start | bytes 8388608
  766.1 5.0 slice-start.1

commit v3 on v2

--- a/solution.py
+++ b/solution.py
@@ -255,6 +255,12 @@
     span_own = span_wide[:, halo : halo + z_cols]
 
     blocks = fluid_temp.reshape(z_rows, n_mode, rows_y * n_x).transpose(1, 0, 2)
+    conduct = jnp.where(
+        material == 0, 0.5, jnp.where(material == 1, 1.0, jnp.where(material == 2, 2.0, 4.0))
+    ).astype(jnp.float32)
+    both = jnp.concatenate(padded(jnp.stack([solid_temp, conduct]), "mode", 2, halo), axis=2)
+    before, both, after = padded(both, "tile", 4, halo)
+    blocks, before, both, after = lax.optimization_barrier((blocks, before, both, after))
     fluid = lax.all_to_all(blocks, "mode", split_axis=0, concat_axis=0, tiled=True)
     codes, scales = span_transform(
         jnp.asarray(split_table(SIGMA * span)), fluid.reshape(n_z, rows_y * n_x), rows_y
@@ -294,11 +300,6 @@
     wall_eigen = jnp.asarray(sine_eigen(n_y), jnp.float32)[:, None]
     fluid_modes = helmholtz(spectra, wall_hat, eigen, wall_eigen, tables)
 
-    conduct = jnp.where(
-        material == 0, 0.5, jnp.where(material == 1, 1.0, jnp.where(material == 2, 2.0, 4.0))
-    ).astype(jnp.float32)
-    both = jnp.concatenate(padded(jnp.stack([solid_temp, conduct]), "mode", 2, halo), axis=2)
-    before, both, after = padded(both, "tile", 4, halo)
     filling = jnp.ones(both.shape[:4] + (128 - 2 * halo,), jnp.float32)
     both = jnp.concatenate([both, after, filling, before], axis=4)
     thermal = conduct_walls(both[0], both[1], z_cols)

time: 785 us -> 694 us (0.88)
  starting transfers between devices: 110 us -> 22 us
  local copies, waits for them, and re-layouts: 91.7 us -> 100 us
    all_to_all x1, starting transfers between devices: 96.1 us -> 8.31 us  [per_device(): near = lax.all_to_all(near, BOTH, split_axis=0, concat_axis=0, tiled=True)]
    ppermute x2, waiting for transfers between devices: 109 us -> 45.4 us  [padded(): lax.ppermute(last, axis, up)]
    all_to_all x1, waiting for transfers between devices: 0.01 us -> 55.2 us  [per_device(): codes = lax.all_to_all(codes, BOTH, split_axis=0, concat_axis=0, tiled=True)]
    concatenate x0 -> x1, other arithmetic: none -> 10.3 us  [per_device(): jnp.concatenate(padded(jnp.stack([solid_temp, conduct]), 'mode', 2, halo)...]
    slice x1 -> x2, local copies, waits for them, and re-layouts: 3.47 us -> 13.3 us  [padded(): first = lax.slice_in_dim(array, 0, width, axis=dim)]
    slice x1 -> x0, other arithmetic: 7.92 us -> none  [padded(): first = lax.slice_in_dim(array, 0, width, axis=dim)]
    unnamed x40 -> x42, local copies, waits for them, and re-layouts: 22.4 us -> 23.9 us
  transfers between devices with their start and end apart: 7 -> 7, of which waited for: 5 -> 5; matrix products, arithmetic and copies ran while one was open for 10% -> 11% of each run, Pallas kernels for 11% -> 12%
where the time goes in v3:
time: 694 us; the launch traced here: 685 us
  waiting for transfers between devices  265 us (38%)
  Pallas kernels  164 us (24%)
  local copies, waits for them, and re-layouts  100 us (14%)
  other arithmetic  71.8 us (10%)
  blocking collectives  51.5 us (7%)
  starting transfers between devices  22 us (3%)
  matrix products  10.1 us (1%)
    all_to_all x1, waiting for transfers between devices, per_device(): lax.all_to_all(blocks, 'mode', split_axis=0, concat_axis=0, tiled=True)  146 us
    pallas_call x1, Pallas kernels, conduct_walls(): pl.pallas_call(conduct_kernel, grid=(walls,), in_specs=[block, block], ou...  82.9 us
    pallas_call x1, Pallas kernels, helmholtz(): pl.pallas_call(helmholtz_kernel, grid=(modes,), in_specs=[each(spectra),...  56.5 us
    all_to_all x1, waiting for transfers between devices, per_device(): codes = lax.all_to_all(codes, BOTH, split_axis=0, concat_axis=0, tiled=True)  55.2 us
    all_to_all x1, blocking collectives, per_device(): small = lax.all_to_all(small, BOTH, split_axis=0, concat_axis=0, tiled=True)  51.5 us
    ppermute x2, waiting for transfers between devices, padded(): lax.ppermute(last, axis, up)  45.4 us
    reshape x2, local copies, waits for them, and re-layouts, per_device(): blocks = fluid_temp.reshape(z_rows, n_mode, rows_y * n_x).transpose(1, 0, 2)  24.8 us
    pallas_call x1, Pallas kernels, span_transform(): pl.pallas_call(functools.partial(span_kernel, rows_y, width // rows_y), g...  24.4 us
  transfers between devices with their start and end apart: 7, of which 5 were waited for; matrix products, arithmetic and copies ran while one was open for 11% of the time, Pallas kernels for 12%

profile of v3, /device:TPU:1, one launch (start us, length us, event | category | flops | bytes accessed | tf_op | source)
XLA Modules:
  0.0 685.3 jit_solution(10976300848209190555)
XLA Ops:
  0.6 4.4 select_bitcast_fusion
  9.6 45.4 %collective-permute-done = f32[2,2,4,64,512]{4,3,2,1,0:T(8,128)S(1)} collective-permute-done((f32[2,2,4,64,512]{4,3,2,1,0:T(8,128)S(1)}, f32[2,2,4,64,512]{4,3,2,1,0:T(8,128)S(1)}, u32[]{:S(2)}, u32[]{:S(2)}) %collective-permute-start) | collective-permute-done | bytes 2097184 | tf_op jit(solution)/shard_map/ppermute | solution.py:148
  57.5 10.3 %pad_maximum_fusion.1 = f32[2,2,40,64,512]{4,3,2,1,0:T(8,128)} fusion(f32[2,2,4,64,512]{4,3,2,1,0:T(8,128)S(1)} %collective-permute-done.1, f32[1,2,32,64,512]{4,3,2,1,0:T(8,128)S(1)} %select_bitcast_fusion, f32[1,2,32,64,512]{4,3,2,1,0:T(8,128)S(1)} %bitcast.58, f32[2,2,4,64,512]{4,3,2,1,0:T(8,128)S(1)} %collective-permute-done), kind=kLoop, calls=%fused_computation.1 | loop fusion | flops 15728640 | bytes 41943040 | tf_op jit(solution)/shard_map/concatenate | solution.py:261
  67.8 9.8 %fusion.74 = (f32[2,2,40,64,4]{4,3,2,1,0:T(8,128)}, f32[2,2,40,64,4]{4,3,2,1,0:T(8,128)}) fusion(f32[2,2,40,64,512]{4,3,2,1,0:T(8,128)} %pad_maximum_fusion.1), kind=kLoop, calls=%fused_computation.160 | loop fusion | bytes 655360 | tf_op jit(solution)/shard_map/slice | solution.py:147
  86.1 13.4 %reshape.122 = bf16[64,16,4096]{2,1,0:T(8,128)(2,1)} reshape(bf16[64,128,512]{2,1,0:T(8,128)(2,1)} %param.12) | data formatting | bytes 16777216 | tf_op jit(solution)/shard_map/reshape | solution.py:257
  99.5 11.4 %copy.55 = bf16[64,16,4096]{2,0,1:T(8,128)(2,1)} copy(bf16[64,16,4096]{2,1,0:T(8,128)(2,1)} %reshape.122) | data formatting | bytes 16777216 | tf_op jit(solution)/shard_map/reshape | solution.py:257
  110.9 5.9 all-to-all-start
  121.3 146.4 %all-to-all-done = bf16[16,64,4096]{2,1,0:T(8,128)(2,1)} async-done(((bf16[16,64,4096]{2,1,0:T(8,128)(2,1)}), bf16[16,64,4096]{2,1,0:T(8,128)(2,1)}, u32[]{:S(2)}, u32[]{:S(2)}) %all-to-all-start) | async-done | bytes 8388640 | tf_op jit(solution)/shard_map/all_to_all | solution.py:264
  269.9 24.4 %shard_map.131 = (s16[1024,4096]{1,0:T(8,128)(2,1)}, f32[1024,128]{1,0:T(8,128)S(1)}) custom-call(bf16[2,1024,1024]{2,1,0:T(8,128)(2,1)S(1)} %copy-done, bf16[1024,4096]{1,0:T(8,128)(2,1)} %bitcast.3.fluid_ref), custom_call_target="tpu_custom_call" | custom-call | flops 17179869184 | bytes 16777216 | tf_op jit(solution)/shard_map/pallas_call | solution.py:88
  294.7 51.5 %all_to_all.32 = f32[32,32,72]{2,1,0:T(8,128)S(1)} all-to-all(f32[32,32,72]{2,1,0:T(8,128)S(1)} %bitcast.65), channel_id=1, replica_groups=mesh['mode'=16,'tile'=2] {'mode','tile'}, dimensions={0} | all-to-all | bytes 589824 | tf_op jit(solution)/shard_map/all_to_all | solution.py:273
  363.0 12.1 %pad_maximum_fusion = f32[2,2,40,64,640]{4,3,2,1,0:T(8,128)S(1)} fusion(f32[2,2,40,64,4]{4,3,2,1,0:T(8,128)} %copy.39, f32[2,2,40,64,4]{4,3,2,1,0:T(8,128)S(1)} %bitcast.56, f32[2,2,40,64,512]{4,3,2,1,0:T(8,128)} %pad_maximum_fusion.1, f32[640]{0:T(1024)S(1)} %pad.51.clone), kind=kLoop, calls=%fused_computation | loop fusion | flops 19660800 | bytes 47516160 | tf_op jit(solution)/shard_map/concatenate | solution.py:304
  375.1 9.4 %slice_bitcast_fusion = (f32[2,40,64,640]{3,2,1,0:T(8,128)}, f32[2,40,64,640]{3,2,1,0:T(8,128)}) fusion(f32[2,2,40,64,640]{4,3,2,1,0:T(8,128)S(1)} %pad_maximum_fusion), kind=kLoop, calls=%fused_computation.4 | loop fusion | bytes 52428800 | tf_op jit(solution)/shard_map/squeeze | solution.py:305
  384.4 82.9 %shard_map.133 = f32[2,32,64,512]{3,2,1,0:T(8,128)} custom-call(f32[2,40,64,640]{3,2,1,0:T(8,128)} %get-tuple-element.15.thermal_ref, f32[2,40,64,640]{3,2,1,0:T(8,128)} %get-tuple-element.14.conduct_ref), custom_call_target="tpu_custom_call" | custom-call | flops 1048576000 | bytes 39321600 | tf_op jit(solution)/shard_map/pallas_call | solution.py:219
  467.3 8.2 %slice.444 = f32[2,32,60,512]{3,2,1,0:T(8,128)} slice(f32[2,32,64,512]{3,2,1,0:T(8,128)} %shard_map.133), slice={[0:2], [0:32], [4:64], [0:512]} | slice | bytes 15728640 | tf_op jit(solution)/shard_map/slice | solution.py:334
  477.4 55.2 %all-to-all-done.1 = s16[32,32,4096]{2,1,0:T(8,128)(2,1)} async-done(((s16[32,32,4096]{2,1,0:T(8,128)(2,1)}), s16[32,32,4096]{2,1,0:T(8,128)(2,1)}, u32[]{:S(2)}, u32[]{:S(2)}) %all-to-all-start.1) | async-done | bytes 8388640 | tf_op jit(solution)/shard_map/all_to_all | solution.py:274
  532.5 12.4 %convert.1 = f32[128,8,8,512]{3,1,2,0:T(8,128)} convert(s16[128,8,8,512]{3,1,2,0:T(8,128)(2,1)} %bitcast.42) | non-fusion elementwise | flops 4194304 | bytes 25165824
  545.0 19.3 %copy.47 = f32[128,8,8,512]{3,2,1,0:T(8,128)S(1)} copy(f32[128,8,8,512]{3,1,2,0:T(8,128)} %convert.1) | data formatting | bytes 33554432
  564.3 6.2 fusion.spectra_ref
  570.6 56.5 %shard_map.132 = f32[32,256,512]{2,1,0:T(8,128)} custom-call(f32[32,256,512]{2,1,0:T(8,128)} %fusion.spectra_ref, f32[32,2,512]{2,1,0:T(2,128)S(1)} %reshape.127.wall_ref, f32[32,1,512]{2,1,0:T(1,128)S(1)} %broadcast_add_fusion.eigen_ref, f32[256,1]{1,0:T(8,128)S(1)} %copy-done.5, bf16[2,256,256]{2,1,0:T(8,128)(2,1)S(1)} %copy-done.4, ...), custom_call_target="tpu_custom_call" | custom-call | flops 38654705664 | bytes 33554432 | tf_op jit(solution)/shard_map/pallas_call | solution.py:126
  632.2 8.3 %all-to-all-start.3 = ((f32[32,32,80]{2,1,0:T(8,128)}), f32[32,32,80]{2,1,0:T(8,128)}, u32[]{:S(2)}, u32[]{:S(2)}) async-start(f32[32,32,80]{2,1,0:T(8,128)} %bitcast.15), calls=%async_computation.3 | async-start | bytes 1048576 | tf_op jit(solution)/shard_map/all_to_all | solution.py:322
  641.2 15.0 %all-to-all-done.3 = f32[32,32,80]{2,1,0:T(8,128)} async-done(((f32[32,32,80]{2,1,0:T(8,128)}), f32[32,32,80]{2,1,0:T(8,128)}, u32[]{:S(2)}, u32[]{:S(2)}) %all-to-all-start.3) | async-done | bytes 327712 | tf_op jit(solution)/shard_map/all_to_all | solution.py:322
  658.8 6.9 %fusion.10 = f32[2,40,520]{2,1,0:T(8,128)S(1)} fusion(f32[1024,1032]{0,1:T(8,128)} %constant.19.clone, s32[]{:T(128)S(6)} %select_n.20, f32[1024,2,40]{2,1,0:T(2,128)} %reshape.128, f32[2,40,4,520]{3,1,0,2:T(8,128)} %bitcast.67), kind=kOutput, calls=%fused_computation.27 | convolution fusion | flops 511264000 | bytes 3549700 | tf_op jit(solution)/shard_map/mwx,mz->wxz/dot_general | solution.py:323
  676.2 4.1 fusion.43
  680.4 4.7 pad_maximum_fusion.2
  (105 shorter events, 59.8 us)
Async XLA Ops:
  0.6 5.8 copy-start.6
  6.9 48.1 %collective-permute-start = (f32[2,2,4,64,512]{4,3,2,1,0:T(8,128)S(1)}, f32[2,2,4,64,512]{4,3,2,1,0:T(8,128)S(1)}, u32[]{:S(2)}, u32[]{:S(2)}) collective-permute-start(f32[2,2,4,64,512]{4,3,2,1,0:T(8,128)S(1)} %get-tuple-element.20), channel_id=1, source_target_pairs={{0,2},{2,4},{4,6},{6,8},{8,10},{10,12},{12,14},{14,16},{16,18},{18... | collective-permute-start | bytes 6291464 | tf_op jit(solution)/shard_map/ppermute | solution.py:148
  9.6 47.9 %collective-permute-start.1 = (f32[2,2,4,64,512]{4,3,2,1,0:T(8,128)S(1)}, f32[2,2,4,64,512]{4,3,2,1,0:T(8,128)S(1)}, u32[]{:S(2)}, u32[]{:S(2)}) collective-permute-start(f32[2,2,4,64,512]{4,3,2,1,0:T(8,128)S(1)} %get-tuple-element.21), channel_id=1, source_target_pairs={{2,0},{4,2},{6,4},{8,6},{10,8},{12,10},{14,12},{16,14},{18,16},{20... | collective-permute-start | bytes 6291464 | tf_op jit(solution)/shard_map/ppermute | solution.py:148
  84.6 26.3 %collective-permute-start.2 = (f32[2,2,40,64,4]{3,2,4,1,0:T(8,128)S(1)}, f32[2,2,40,64,4]{3,2,4,1,0:T(8,128)S(1)}, u32[]{:S(2)}, u32[]{:S(2)}) collective-permute-start(f32[2,2,40,64,4]{3,2,4,1,0:T(8,128)S(1)} %copy.30), channel_id=1, source_target_pairs={{0,1},{1,0},{2,3},{3,2},{4,5},{5,4},{6,7},{7,6},{8,9},{9,8},{10,11... | collective-permute-start | bytes 491528 | tf_op jit(solution)/shard_map/ppermute | solution.py:148
  85.8 25.1 %collective-permute-start.3 = (f32[2,2,40,64,4]{3,2,4,1,0:T(8,128)S(1)}, f32[2,2,40,64,4]{3,2,4,1,0:T(8,128)S(1)}, u32[]{:S(2)}, u32[]{:S(2)}) collective-permute-start(f32[2,2,40,64,4]{3,2,4,1,0:T(8,128)S(1)} %copy.31), channel_id=1, source_target_pairs={{1,0},{0,1},{3,2},{2,3},{5,4},{4,5},{7,6},{6,7},{9,8},{8,9},{11,10... | collective-permute-start | bytes 491528 | tf_op jit(solution)/shard_map/ppermute | solution.py:148
  110.9 156.9 %all-to-all-start = ((bf16[16,64,4096]{2,1,0:T(8,128)(2,1)}), bf16[16,64,4096]{2,1,0:T(8,128)(2,1)}, u32[]{:S(2)}, u32[]{:S(2)}) async-start(bf16[16,64,4096]{2,1,0:T(8,128)(2,1)} %bitcast.61), calls=%async_computation | async-start | bytes 16777216 | tf_op jit(solution)/shard_map/all_to_all | solution.py:264
  267.7 2.2 copy-start
  346.2 4.4 copy-start.7
  346.2 186.3 %all-to-all-start.1 = ((s16[32,32,4096]{2,1,0:T(8,128)(2,1)}), s16[32,32,4096]{2,1,0:T(8,128)(2,1)}, u32[]{:S(2)}, u32[]{:S(2)}) async-start(s16[32,32,4096]{2,1,0:T(8,128)(2,1)} %bitcast.62), calls=%async_computation.1 | async-start | bytes 16777216 | tf_op jit(solution)/shard_map/all_to_all | solution.py:274
  357.2 5.8 slice-start
  358.5 4.5 slice-start.1
  564.3 6.3 copy-start.1
  564.3 6.3 copy-start.2
  564.3 6.3 copy-start.3
  564.3 6.2 copy-start.4
  564.3 6.2 copy-start.5
  632.2 24.0 %all-to-all-start.3 = ((f32[32,32,80]{2,1,0:T(8,128)}), f32[32,32,80]{2,1,0:T(8,128)}, u32[]{:S(2)}, u32[]{:S(2)}) async-start(f32[32,32,80]{2,1,0:T(8,128)} %bitcast.15), calls=%async_computation.3 | async-start | bytes 1048576 | tf_op jit(solution)/shard_map/all_to_all | solution.py:322
  671.6 8.7 %slice-start.2 = ((s8[8388608]{0:T(1024)(128)(4,1)}), s8[4194304]{0:T(1024)(128)(4,1)S(1)}, s32[]{:S(2)}) async-start(s8[8388608]{0:T(1024)(128)(4,1)} %bitcast.59), calls=%async_computation.6 | async-start | bytes 8388608
  675.3 5.0 slice-start.3
